TPU v7x, 512 devices: a whole 4x8x8 slice. The times are simulated.
512 devices in a mesh: blk: 4 (over x), dp: 128 (over z, y, core).
Axes of the slice: x: 4, y: 8, z: 8, core: 2. Of those that a mesh axis runs over, the one named last changes fastest.
Arguments:
- q_raw: bfloat16 [65536, 2048], P(('dp', 'blk')), may hold values from -6 to 6
- k_raw: bfloat16 [65536, 2048], P(('dp', 'blk')), may hold values from -6 to 6
- values: bfloat16 [65536, 2048], P(('dp', 'blk')), may hold values from -6 to 6
- grad_out: bfloat16 [65536, 2048], P(('dp', 'blk')), may hold values from -6 to 6
- q_gain: float32 [2048], replicated, may hold values from 0.5 to 5.5
- k_gain: float32 [2048], replicated, may hold values from 0.5 to 5.5
- patch_counts: int32 [512], replicated, may hold values from 0 to 512, as said below
- assignment: int32 [512], replicated, may hold values from 0 to 127, as said below
- loader_shard: int32 [512], replicated, may hold values from 0 to 127
Outputs:
- attended: bfloat16 [65536, 2048], P(('dp', 'blk'))
- q_grad: bfloat16 [65536, 2048], P(('dp', 'blk'))
- k_grad: bfloat16 [65536, 2048], P(('dp', 'blk'))
- v_grad: bfloat16 [65536, 2048], P(('dp', 'blk'))
- q_gain_grad: float32 [2048], replicated
- k_gain_grad: float32 [2048], replicated
Inputs may be any that keep to these rules, and one draw needn't show every extreme that they name: `patch_counts`: an entry of 0 is no image; every other count is 128 or more; the counts of the entries assigned to one group sum to 512; each group has 1 to half of 4 images; some image fills a whole group. `assignment`: every group is named by some entry with a positive count.
All inputs are finite; a program needn't handle non-finite values.
Results may differ from a plain program's by a relative error of at most 0.04.
The roundings to bfloat16 on the way count: a program that leaves them out, or rounds other values in their place, can miss the bound.
Values may be sent and summed in bfloat16 or wider, within the bound.
No kernel may reach another device: no remote copies, remote signals or barrier semaphores. Data moves between devices by JAX's collectives and lax.ppermute only.
A program may use at most 64 MiB of HBM per device.

v0:
```python
import jax
import jax.numpy as jnp
from jax import lax
from jax.sharding import PartitionSpec as P

HEAD_DIM = 128


epsilon = 1e-06
masked_score = -1e30


def image_weights(patch_counts, loader_shard, group_count):
    living = patch_counts > 0
    shared = (loader_shard[:, None] == loader_shard[None, :]) & living[None, :]
    per_loader = jnp.sum(shared.astype(jnp.int32), axis=1)
    per_loader = jnp.where(living, per_loader, 1)
    living_total = jnp.sum(living.astype(jnp.int32))
    return living_total.astype(jnp.float32) / (group_count * per_loader).astype(jnp.float32)


def row_layout(patch_counts, assignment, image_weight, group_index, first_row, row_total):
    owned = jnp.where(assignment == group_index, patch_counts, 0)
    offsets = jnp.cumsum(owned) - owned
    positions = first_row + jnp.arange(row_total, dtype=jnp.int32)
    inside = (positions[:, None] >= offsets[None, :]) & (
        positions[:, None] < (offsets + owned)[None, :]
    )
    entries = jnp.arange(patch_counts.shape[0], dtype=jnp.int32)
    segments = jnp.sum(jnp.where(inside, entries[None, :], 0), axis=1)
    row_weight = jnp.sum(jnp.where(inside, image_weight[None, :], 0.0), axis=1)
    return (segments, row_weight)


def normed(raw, gain):
    widened = raw.astype(jnp.float32)
    inverse = lax.rsqrt(jnp.mean(widened * widened, axis=-1, keepdims=True) + epsilon)
    unit_rows = widened * inverse
    return (unit_rows, inverse, (unit_rows * gain).astype(jnp.bfloat16))


def norm_back(grad_normed, unit_rows, inverse, gain):
    grad_unit = grad_normed * gain
    grad_raw = inverse * (
        grad_unit - unit_rows * jnp.mean(grad_unit * unit_rows, axis=-1, keepdims=True)
    )
    return (grad_raw.astype(jnp.bfloat16), jnp.sum(grad_normed * unit_rows, axis=0))


def split_heads(array, head_count):
    return array.reshape(array.shape[0], head_count, HEAD_DIM)


def forward_rows(query_rows, grad_rows, key_all, value_all, same_image, score_scale):
    scores = (
        jnp.einsum("qhd,khd->qhk", query_rows, key_all, preferred_element_type=jnp.float32)
        * score_scale
    )
    scores = jnp.where(same_image[:, None, :], scores, masked_score)
    row_max = jnp.max(scores, axis=2, keepdims=True)
    log_total = row_max + jnp.log(jnp.sum(jnp.exp(scores - row_max), axis=2, keepdims=True))
    softmax = jnp.where(same_image[:, None, :], jnp.exp(scores - log_total), 0.0)
    softmax_half = softmax.astype(jnp.bfloat16)
    attended_block = jnp.einsum(
        "qhk,khd->qhd", softmax_half, value_all, preferred_element_type=jnp.float32
    )
    grad_scores = jnp.einsum(
        "qhd,khd->qhk", grad_rows, value_all, preferred_element_type=jnp.float32
    )
    row_delta = jnp.sum(grad_rows.astype(jnp.float32) * attended_block, axis=2, keepdims=True)
    weighted_half = (softmax * grad_scores).astype(jnp.bfloat16)
    query_grad = score_scale * (
        jnp.einsum("qhk,khd->qhd", weighted_half, key_all, preferred_element_type=jnp.float32)
        - row_delta
        * jnp.einsum("qhk,khd->qhd", softmax_half, key_all, preferred_element_type=jnp.float32)
    )
    return (softmax, softmax_half, grad_scores, row_delta, attended_block, query_grad, log_total)


def body(q_raw, k_raw, values, grad_out, q_gain, k_gain, patch_counts, assignment, loader_shard):
    row_count, model_width = q_raw.shape
    head_count = model_width // HEAD_DIM
    cycle_size = lax.axis_size("blk")
    group_count = lax.axis_size("dp")
    group_index = lax.axis_index("dp")
    cycle_index = lax.axis_index("blk")
    score_scale = HEAD_DIM ** (-0.5)
    image_weight = image_weights(patch_counts, loader_shard, group_count)
    own_segments, row_weight = row_layout(
        patch_counts, assignment, image_weight, group_index, cycle_index * row_count, row_count
    )
    query_unit, query_inverse, query_normed = normed(q_raw, q_gain)
    key_unit, key_inverse, key_normed = normed(k_raw, k_gain)
    grad_weighted = (grad_out.astype(jnp.float32) * row_weight[:, None]).astype(jnp.bfloat16)
    group_rows = row_count * cycle_size

    def segments_at(piece_start, piece_rows):
        return row_layout(
            patch_counts, assignment, image_weight, group_index, piece_start, piece_rows
        )[0]

    query_three = split_heads(query_normed, head_count)
    grad_three = split_heads(grad_weighted, head_count)
    key_three = split_heads(key_normed, head_count)
    value_three = split_heads(values, head_count)
    shard_piece = (
        lax.all_gather(key_normed, "blk", axis=0, tiled=True),
        lax.all_gather(values, "blk", axis=0, tiled=True),
    )
    key_buffer = shard_piece[0]
    value_buffer = shard_piece[1]
    key_all = split_heads(key_buffer, head_count)
    value_all = split_heads(value_buffer, head_count)
    group_segments = segments_at(jnp.int32(0), group_rows)
    same_image = own_segments[:, None] == group_segments[None, :]
    softmax, softmax_half, grad_scores, row_delta3, attended_full, query_grad, log_total3 = (
        forward_rows(query_three, grad_three, key_all, value_all, same_image, score_scale)
    )
    log_total = log_total3[:, :, 0]
    row_delta = row_delta3[:, :, 0]
    total_all, delta_all = (
        lax.all_gather(log_total, "blk", axis=0, tiled=True),
        lax.all_gather(row_delta, "blk", axis=0, tiled=True),
    )
    shard_piece = (
        lax.all_gather(query_normed, "blk", axis=0, tiled=True),
        lax.all_gather(grad_weighted, "blk", axis=0, tiled=True),
    )
    piece_rows = shard_piece[0].shape[0]
    query_piece = split_heads(shard_piece[0], head_count)
    grad_piece = split_heads(shard_piece[1], head_count)
    same_piece = segments_at(jnp.int32(0), piece_rows)[:, None] == own_segments[None, :]
    scores = (
        jnp.einsum("qhd,khd->qhk", query_piece, key_three, preferred_element_type=jnp.float32)
        * score_scale
    )
    softmax_piece = jnp.where(same_piece[:, None, :], jnp.exp(scores - total_all[:, :, None]), 0.0)
    grad_piece_scores = jnp.einsum(
        "qhd,khd->qhk", grad_piece, value_three, preferred_element_type=jnp.float32
    )
    score_grad_half = (softmax_piece * (grad_piece_scores - delta_all[:, :, None])).astype(
        jnp.bfloat16
    )
    key_sums = score_scale * jnp.einsum(
        "qhk,qhd->khd", score_grad_half, query_piece, preferred_element_type=jnp.float32
    )
    value_sums = jnp.einsum(
        "qhk,qhd->khd",
        softmax_piece.astype(jnp.bfloat16),
        grad_piece,
        preferred_element_type=jnp.float32,
    )
    key_sums, value_sums = (key_sums, value_sums)
    attended = attended_full.reshape(row_count, model_width).astype(jnp.bfloat16)
    query_grad_normed = query_grad.reshape(row_count, model_width)
    key_grad_normed = key_sums.reshape(row_count, model_width)
    v_grad = value_sums.reshape(row_count, model_width).astype(jnp.bfloat16)
    q_grad, q_part = norm_back(query_grad_normed, query_unit, query_inverse, q_gain)
    k_grad, k_part = norm_back(key_grad_normed, key_unit, key_inverse, k_gain)
    q_gain_grad, k_gain_grad = lax.psum((q_part, k_part), ("blk", "dp"))
    return (attended, q_grad, k_grad, v_grad, q_gain_grad, k_gain_grad)


def solution(mesh):
    placed = (
        P(("dp", "blk"), None),
        P(("dp", "blk"), None),
        P(("dp", "blk"), None),
        P(("dp", "blk"), None),
        P(),
        P(),
        P(),
        P(),
        P(),
    )
    return jax.shard_map(
        body,
        mesh=mesh,
        in_specs=placed,
        out_specs=(
            P(("dp", "blk"), None),
            P(("dp", "blk"), None),
            P(("dp", "blk"), None),
            P(("dp", "blk"), None),
            P(),
            P(),
        ),
        check_vma=False,
    )
```

profile of v0, /device:TPU:1, one launch (start us, length us, event | category | flops | bytes accessed | tf_op | source)
XLA Modules:
  0.0 298.1 jit_solution(8691059399919728748)
XLA Ops:
  8.0 1.3 copy.75
  9.6 1.8 fusion.28
  11.5 1.3 copy.76
  13.1 1.1 fusion.35
  18.3 33.5 %all-gather.7.cloned.1.call-done = bf16[512,2048]{1,0:T(8,128)(2,1)} async-done(((bf16[128,2048]{1,0:T(8,128)(2,1)}), bf16[512,2048]{1,0:T(8,128)(2,1)}) %all-gather.7.cloned.1.call-update) | async-done | bytes 2097168 | tf_op jit(solution)/shard_map/all_gather | solution.py:108
  51.8 2.9 copy.79
  54.7 38.9 %all-gather.5.cloned.1.call-done = bf16[512,2048]{0,1:T(8,128)(2,1)} async-done(((bf16[128,2048]{0,1:T(8,128)(2,1)}), bf16[512,2048]{0,1:T(8,128)(2,1)}) %all-gather.5.cloned.1.call-update) | async-done | bytes 2097168 | tf_op jit(solution)/shard_map/all_gather | solution.py:107
  93.6 2.8 fusion.7
  97.3 2.6 multiply_reduce_fusion
  100.0 2.0 copy.94
  102.1 5.1 %fusion.14 = f32[128,16,128]{0,2,1:T(8,128)} fusion(bf16[512,16,128]{0,2,1:T(8,128)(2,1)} %bitcast.120, f32[128,16]{0,1:T(8,128)S(1)} %get-tuple-element.36, f32[16,512,128]{2,1,0:T(8,128)} %copy-done, f32[128,16]{0,1:T(8,128)S(1)} %log_add_fusion, pred[128,512]{0,1:T(8,128)(4,1)S(1)} %broadcast_compare_fusion.1), kind=kOutput, calls=%fused_computation.22 | convolution fusion | flops 273940480 | bytes 7421952 | tf_op jit(solution)/shard_map/qhk,khd->qhd/dot_general | solution.py:75
  107.2 6.4 %fusion.16 = f32[128,16,128]{0,2,1:T(8,128)} fusion(f32[128,16,128]{0,2,1:T(8,128)} %fusion.14, bf16[512,16,128]{0,2,1:T(8,128)(2,1)} %bitcast.121, f32[16,512,128]{2,1,0:T(8,128)} %copy-done, bf16[128,16,128]{0,2,1:T(8,128)(2,1)} %bitcast.115, bf16[512,16,128]{0,2,1:T(8,128)(2,1)S(1)} %bitcast.112, f32[128,16]{0,1:T(8,128)S(1)} %log_add_fusion, ...), kind=kOutput, calls=%fused_computation.25 | convolution fusion | flops 543686656 | bytes 11083776 | tf_op jit(solution)/shard_map/qhk,khd->qhd/dot_general | solution.py:73
  113.6 1.9 fusion.40
  115.5 1.6 fusion.39
  117.1 1.0 copy.95
  118.1 9.8 %all_gather.23 = f32[512,16]{0,1:T(8,128)S(1)} all-gather(f32[128,16]{0,1:T(8,128)S(1)} %get-tuple-element.36), channel_id=1, replica_groups=mesh['blk'=4,'dp'=128] {'blk'}, dimensions={0}, use_global_device_ids=true | all-gather | bytes 40960 | tf_op jit(solution)/shard_map/all_gather | solution.py:123
  127.9 9.6 %all_gather.21 = f32[512,16]{0,1:T(8,128)S(1)} all-gather(f32[128,16]{0,1:T(8,128)S(1)} %log_add_fusion), channel_id=1, replica_groups=mesh['blk'=4,'dp'=128] {'blk'}, dimensions={0}, use_global_device_ids=true | all-gather | bytes 40960 | tf_op jit(solution)/shard_map/all_gather | solution.py:122
  137.5 4.3 %fusion.58 = f32[16,128,512]{2,1,0:T(8,128)} fusion(bf16[128,16,128]{0,2,1:T(8,128)(2,1)S(1)} %bitcast.113, bf16[512,16,128]{0,2,1:T(8,128)(2,1)} %bitcast.117), kind=kOutput, calls=%fused_computation.90 | convolution fusion | flops 268435456 | bytes 6815744 | tf_op jit(solution)/shard_map/qhd,khd->qhk/dot_general | solution.py:134
  141.8 38.6 %all-gather.11.cloned.1.call-done = bf16[512,2048]{0,1:T(8,128)(2,1)} async-done(((bf16[128,2048]{0,1:T(8,128)(2,1)}), bf16[512,2048]{0,1:T(8,128)(2,1)}) %all-gather.11.cloned.1.call-update) | async-done | bytes 2097168 | tf_op jit(solution)/shard_map/all_gather | solution.py:127
  180.3 3.8 %fusion.25 = bf16[16,128,128]{2,1,0:T(8,128)(2,1)S(1)} fusion(bf16[512,16,128]{0,2,1:T(8,128)(2,1)} %bitcast.123, f32[16,128,512]{2,1,0:T(8,128)} %fusion.58, f32[512,16]{0,1:T(8,128)S(1)} %all_gather.21, pred[512,128]{0,1:T(8,128)(4,1)S(1)} %broadcast_compare_fusion), kind=kOutput, calls=%fused_computation.38 | convolution fusion | flops 272891904 | bytes 6914048 | tf_op jit(solution)/shard_map/qhk,qhd->khd/dot_general | solution.py:147
  184.2 5.4 %convolution_multiply_fusion = f32[16,128,128]{2,1,0:T(8,128)S(1)} fusion(bf16[512,16,128]{0,2,1:T(8,128)(2,1)} %bitcast.118, f32[16,128,512]{2,1,0:T(8,128)} %fusion.58, bf16[512,16,128]{0,2,1:T(8,128)(2,1)} %bitcast.124, f32[512,16]{0,1:T(8,128)S(1)} %all_gather.23, f32[512,16]{0,1:T(8,128)S(1)} %all_gather.21, ...), kind=kOutput, calls=%fused_computation.20 | convolution fusion | flops 543424512 | bytes 10092544 | tf_op jit(solution)/shard_map/qhk,qhd->khd/dot_general | solution.py:144
  190.6 1.0 copy.96
  191.6 1.0 copy.97
  192.6 98.9 %all-reduce = (f32[2048]{0:T(1024)}, f32[2048]{0:T(1024)}) all-reduce(f32[2048]{0:T(1024)S(1)} %get-tuple-element.32, f32[2048]{0:T(1024)S(1)} %get-tuple-element.30), channel_id=1, replica_groups=mesh['blk'=4,'dp'=128] {'blk','dp'}, use_global_device_ids=true, to_apply=%region_15.16 | all-reduce | flops 4096 | bytes 32768 | tf_op jit(solution)/shard_map/psum | solution.py:160
  (54 shorter events, 6.7 us)
Async XLA Ops:
  7.2 6.0 %copy-start.5 = (f32[2048]{0:T(1024)S(1)}, f32[2048]{0:T(1024)}, u32[]{:S(2)}) copy-start(f32[2048]{0:T(1024)} %param.13) | copy-start | bytes 24580
  7.2 7.2 %copy-start.7 = (s32[512]{0:T(512)S(1)}, s32[512]{0:T(512)}, u32[]{:S(2)}) copy-start(s32[512]{0:T(512)} %param.15) | copy-start | bytes 6148
  7.2 7.2 %copy-start.8 = (s32[512]{0:T(512)S(1)}, s32[512]{0:T(512)}, u32[]{:S(2)}) copy-start(s32[512]{0:T(512)} %param.16) | copy-start | bytes 6148
  7.2 9.0 %copy-start.3 = (bf16[128,2048]{1,0:T(8,128)(2,1)S(1)}, bf16[128,2048]{1,0:T(8,128)(2,1)}, u32[]{:S(2)}) copy-start(bf16[128,2048]{1,0:T(8,128)(2,1)} %param.12) | copy-start | bytes 1572868
  7.2 10.2 %copy-start.9 = (s32[512]{0:T(512)S(1)}, s32[512]{0:T(512)}, u32[]{:S(2)}) copy-start(s32[512]{0:T(512)} %param.17) | copy-start | bytes 6148
  7.2 44.6 %all-gather.7.cloned.1.call-start = ((), (), s32[]{:S(2)}) async-start(), calls=%async_computation.1 | async-start | bytes 2621440 | tf_op jit(solution)/shard_map/all_gather | solution.py:108
  8.0 85.6 %all-gather.5.cloned.1.call-start = ((), (), s32[]{:S(2)}) async-start(), calls=%async_computation | async-start | bytes 2621440 | tf_op jit(solution)/shard_map/all_gather | solution.py:107
  11.5 126.0 %all-gather.9.cloned.1.call-start = ((), (), s32[]{:S(2)}) async-start(), calls=%async_computation.2 | async-start | bytes 2621440 | tf_op jit(solution)/shard_map/all_gather | solution.py:126
  14.3 166.0 %all-gather.11.cloned.1.call-start = ((), (), s32[]{:S(2)}) async-start(), calls=%async_computation.3 | async-start | bytes 2621440 | tf_op jit(solution)/shard_map/all_gather | solution.py:127
  93.6 3.7 %copy-start.2 = (bf16[128,2048]{0,1:T(8,128)(2,1)S(1)}, bf16[128,2048]{0,1:T(8,128)(2,1)}, u32[]{:S(2)}) copy-start(bf16[128,2048]{0,1:T(8,128)(2,1)} %copy.81) | copy-start | bytes 1572868
  96.4 3.5 %copy-start = (f32[16,512,128]{2,1,0:T(8,128)}, f32[16,512,128]{2,1,0:T(8,128)S(1)}, u32[]{:S(2)}) copy-start(f32[16,512,128]{2,1,0:T(8,128)S(1)} %get-tuple-element.46) | copy-start | bytes 12582916
  113.6 23.9 %copy-start.1 = (bf16[128,2048]{0,1:T(8,128)(2,1)S(1)}, bf16[128,2048]{0,1:T(8,128)(2,1)}, u32[]{:S(2)}) copy-start(bf16[128,2048]{0,1:T(8,128)(2,1)} %fusion.28) | copy-start | bytes 1572868
  141.8 42.4 %copy-start.4 = (bf16[128,2048]{1,0:T(8,128)(2,1)S(1)}, bf16[128,2048]{1,0:T(8,128)(2,1)}, u32[]{:S(2)}) copy-start(bf16[128,2048]{1,0:T(8,128)(2,1)} %param.11) | copy-start | bytes 1572868
  184.2 5.4 %copy-start.6 = (f32[2048]{0:T(1024)S(1)}, f32[2048]{0:T(1024)}, u32[]{:S(2)}) copy-start(f32[2048]{0:T(1024)} %param.14) | copy-start | bytes 24580
Sparse Core Ops, SparseCore 0:
  10.2 41.6 all-gather.6
  54.5 39.0 all-gather.4
  95.7 41.3 all-gather.8
  139.6 40.7 all-gather.10
where the time goes:
time: 299 us; the launch traced here: 298 us
  blocking collectives  118 us (39%)
  waiting for transfers between devices  112 us (37%)
  matrix products  30.5 us (10%)
  between operations  14.7 us (5%)
  local copies, waits for them, and re-layouts  11.8 us (4%)
  other arithmetic  11.1 us (4%)
    psum x1, blocking collectives, body(): q_gain_grad, k_gain_grad = lax.psum((q_part, k_part), ('blk', 'dp'))  98.9 us
    all_gather x1, waiting for transfers between devices, body(): lax.all_gather(key_normed, 'blk', axis=0, tiled=True)  38.9 us
    all_gather x1, waiting for transfers between devices, body(): lax.all_gather(grad_weighted, 'blk', axis=0, tiled=True)  38.6 us
    all_gather x1, waiting for transfers between devices, body(): lax.all_gather(values, 'blk', axis=0, tiled=True)  33.5 us
    all_gather x1, blocking collectives, body(): lax.all_gather(row_delta, 'blk', axis=0, tiled=True)  9.78 us
    all_gather x1, blocking collectives, body(): lax.all_gather(log_total, 'blk', axis=0, tiled=True)  9.56 us
    unnamed x27, local copies, waits for them, and re-layouts  8.73 us
    dot_general x1, matrix products, forward_rows(): jnp.einsum('qhk,khd->qhd', weighted_half, key_all, preferred_element_type...  6.38 us
  transfers between devices with their start and end apart: 4, of which 3 were waited for; matrix products, arithmetic and copies ran while one was open for 14% of the time, Pallas kernels for 0%

commit v1 on v0

v1 whole, which is shorter than its diff:
```python
import functools

import jax
import jax.numpy as jnp
from jax import lax
from jax.experimental import pallas as pl
from jax.experimental.pallas import tpu as pltpu
from jax.sharding import Mesh, PartitionSpec as P

HEAD_DIM = 128
ROW_STEP = 32

epsilon = 1e-06
masked_score = -1e30
log2_e = 1.4426950408889634


def unit_of(raw):
    widened = raw.astype(jnp.float32)
    inverse = lax.rsqrt(jnp.mean(widened * widened, axis=-1, keepdims=True) + epsilon)
    return widened * inverse, inverse


def group_table(counts, assignment, loader, group_index, group_count):
    shape = counts.shape
    entries = lax.broadcasted_iota(jnp.int32, shape, 0) * shape[1] + lax.broadcasted_iota(
        jnp.int32, shape, 1
    )
    living = counts > 0
    owned = living & (assignment == group_index)
    total = shape[0] * shape[1]
    first = jnp.min(jnp.where(owned, entries, total))
    last = jnp.max(jnp.where(owned, entries, -1))
    boundary = jnp.sum(jnp.where(entries == first, counts, 0))
    living_total = jnp.sum(living.astype(jnp.int32))

    def weight_of(entry):
        shard = jnp.sum(jnp.where(entries == entry, loader, 0))
        shared = jnp.sum((living & (loader == shard)).astype(jnp.int32))
        shared = jnp.full((1, 1), group_count * shared, jnp.int32)
        return jnp.full((1, 1), living_total, jnp.int32).astype(jnp.float32) / shared.astype(jnp.float32)

    return boundary, weight_of(first), weight_of(last)


def pack_kernel(
    group_count, cycle, chunks,
    counts_ref, assignment_ref, loader_ref, q_ref, k_ref, v_ref, g_ref, q_gain_ref, k_gain_ref,
    *rest,
):
    packed_refs, boundary_ref, weight_ref = rest[:chunks], rest[chunks], rest[chunks + 1]
    step = pl.program_id(0)
    rows, width = q_ref.shape

    @pl.when(step == 0)
    def _():
        boundary, weight_first, weight_last = group_table(
            counts_ref[...], assignment_ref[...], loader_ref[...], lax.axis_index(("z", "yc")), group_count
        )
        boundary_ref[0] = boundary
        weight_ref[0:1, :] = jnp.broadcast_to(weight_first, (1, 128))
        weight_ref[1:2, :] = jnp.broadcast_to(weight_last, (1, 128))

    own_first = lax.axis_index("blk") * (rows * pl.num_programs(0)) + step * rows
    position = own_first + lax.broadcasted_iota(jnp.int32, (rows, 1), 0)
    row_weight = jnp.where(position < boundary_ref[0], weight_ref[0:1, 0:1], weight_ref[1:2, 0:1])
    q_normed = (unit_of(q_ref[...])[0] * q_gain_ref[...]).astype(jnp.bfloat16)
    k_normed = (unit_of(k_ref[...])[0] * k_gain_ref[...]).astype(jnp.bfloat16)
    g_weighted = (g_ref[...].astype(jnp.float32) * row_weight).astype(jnp.bfloat16)
    share = width // cycle
    piece = share // chunks
    for a, array in enumerate((q_normed, k_normed, v_ref[...], g_weighted)):
        for d in range(cycle):
            for c in range(chunks):
                start = d * share + c * piece
                packed_refs[c][d, a] = array[:, start : start + piece]


def pack(q_raw, k_raw, values, grad_out, q_gain, k_gain, counts, assignment, loader, cycle, group_count, chunks):
    rows, width = q_raw.shape
    piece = width // cycle // chunks
    row_block = pl.BlockSpec((ROW_STEP, width), lambda i: (i, 0))
    table = pl.BlockSpec(counts.shape, lambda i: (0, 0))
    gain = pl.BlockSpec((1, width), lambda i: (0, 0))
    out = pl.pallas_call(
        functools.partial(pack_kernel, group_count, cycle, chunks),
        grid=(rows // ROW_STEP,),
        in_specs=[table] * 3 + [row_block] * 4 + [gain] * 2,
        out_specs=[pl.BlockSpec((cycle, 4, ROW_STEP, piece), lambda i: (0, 0, i, 0))] * chunks
        + [pl.BlockSpec(memory_space=pltpu.SMEM)],
        out_shape=[jax.ShapeDtypeStruct((cycle, 4, rows, piece), jnp.bfloat16)] * chunks
        + [jax.ShapeDtypeStruct((1,), jnp.int32)],
        scratch_shapes=[pltpu.VMEM((8, 128), jnp.float32)],
        compiler_params=pltpu.CompilerParams(vmem_limit_bytes=32 * 1024 * 1024),
        cost_estimate=pl.CostEstimate(flops=12 * rows * width, bytes_accessed=16 * rows * width, transcendentals=rows),
        name="pack",
    )(counts, assignment, loader, q_raw, k_raw, values, grad_out, q_gain, k_gain)
    return out[:chunks], out[chunks]


def dot(a, b, a_dim, b_dim):
    return lax.dot_general(a, b, (((a_dim,), (b_dim,)), ((), ())), preferred_element_type=jnp.float32)


def attention_kernel(boundary_ref, x_ref, o_ref, part_ref):
    cycle, _, rows, width = x_ref.shape
    slots = cycle * rows
    scale = HEAD_DIM ** (-0.5)
    boundary = boundary_ref[0]
    q, k, v, g = (x_ref[:, a].reshape(slots, width) for a in range(4))
    key_first = lax.broadcasted_iota(jnp.int32, (slots, slots), 0) < boundary
    query_first = lax.broadcasted_iota(jnp.int32, (slots, slots), 1) < boundary
    scores = jnp.where(key_first == query_first, dot(k, q, 1, 1), masked_score)
    top = jnp.max(scores, axis=0, keepdims=True)
    powers = jnp.exp2((scores - top) * (scale * log2_e))
    softmax = powers * (1.0 / jnp.sum(powers, axis=0, keepdims=True))
    softmax_half = softmax.astype(jnp.bfloat16)
    both = dot(jnp.concatenate([v, k], axis=1), softmax_half, 0, 0)
    attended_t, key_mean_t = both[:width], both[width:]
    grad_scores = dot(v, g, 1, 1)
    row_delta = jnp.sum(g.astype(jnp.float32).T * attended_t, axis=0, keepdims=True)
    weighted_half = (softmax * grad_scores).astype(jnp.bfloat16)
    score_grad_half = (softmax * (grad_scores - row_delta)).astype(jnp.bfloat16)
    query_grad = (scale * (dot(k, weighted_half, 0, 0) - row_delta * key_mean_t)).T
    key_grad = scale * dot(score_grad_half, q, 1, 0)
    value_grad = dot(softmax_half, g, 1, 0)
    for a, array in enumerate((attended_t.T, query_grad, key_grad, value_grad)):
        o_ref[:, a] = array.astype(jnp.bfloat16).reshape(cycle, rows, width)
    part_ref[0] = jnp.concatenate(
        [
            jnp.sum(query_grad * q.astype(jnp.float32), axis=0, keepdims=True),
            jnp.sum(key_grad * k.astype(jnp.float32), axis=0, keepdims=True),
        ],
        axis=0,
    )


def attention(boundary, packed):
    cycle, kinds, rows, piece = packed.shape
    heads = piece // HEAD_DIM
    slots = cycle * rows
    block = pl.BlockSpec((cycle, kinds, rows, HEAD_DIM), lambda h: (0, 0, 0, h))
    return pl.pallas_call(
        attention_kernel,
        grid=(heads,),
        in_specs=[pl.BlockSpec(memory_space=pltpu.SMEM), block],
        out_specs=[block, pl.BlockSpec((1, 2, HEAD_DIM), lambda h: (h, 0, 0))],
        out_shape=[
            jax.ShapeDtypeStruct(packed.shape, jnp.bfloat16),
            jax.ShapeDtypeStruct((heads, 2, HEAD_DIM), jnp.float32),
        ],
        compiler_params=pltpu.CompilerParams(vmem_limit_bytes=48 * 1024 * 1024),
        cost_estimate=pl.CostEstimate(
            flops=14 * heads * slots * slots * HEAD_DIM, bytes_accessed=32 * slots * piece,
            transcendentals=heads * slots * slots,
        ),
        name="attention",
    )(boundary, packed)


def finish_kernel(cycle, chunks, *refs):
    back_refs = refs[:chunks]
    q_ref, k_ref, q_gain_ref, k_gain_ref, att_ref, dq_ref, dk_ref, dv_ref = refs[chunks:]

    def whole(a):
        return jnp.concatenate([back_refs[c][d, a] for d in range(cycle) for c in range(chunks)], axis=1)

    def norm_back(grad_normed, raw, gain):
        unit, inverse = unit_of(raw)
        grad_unit = grad_normed.astype(jnp.float32) * gain
        mean = jnp.mean(grad_unit * unit, axis=-1, keepdims=True)
        return (inverse * (grad_unit - unit * mean)).astype(jnp.bfloat16)

    att_ref[...] = whole(0)
    dq_ref[...] = norm_back(whole(1), q_ref[...], q_gain_ref[...])
    dk_ref[...] = norm_back(whole(2), k_ref[...], k_gain_ref[...])
    dv_ref[...] = whole(3)


def finish(back, q_raw, k_raw, q_gain, k_gain):
    rows, width = q_raw.shape
    cycle, kinds, _, piece = back[0].shape
    row_block = pl.BlockSpec((ROW_STEP, width), lambda i: (i, 0))
    gain = pl.BlockSpec((1, width), lambda i: (0, 0))
    return pl.pallas_call(
        functools.partial(finish_kernel, cycle, len(back)),
        grid=(rows // ROW_STEP,),
        in_specs=[pl.BlockSpec((cycle, kinds, ROW_STEP, piece), lambda i: (0, 0, i, 0))] * len(back)
        + [row_block] * 2 + [gain] * 2,
        out_specs=[row_block] * 4,
        out_shape=[jax.ShapeDtypeStruct((rows, width), jnp.bfloat16)] * 4,
        compiler_params=pltpu.CompilerParams(vmem_limit_bytes=32 * 1024 * 1024),
        cost_estimate=pl.CostEstimate(flops=20 * rows * width, bytes_accessed=20 * rows * width, transcendentals=rows),
        name="finish",
    )(*back, q_raw, k_raw, q_gain, k_gain)


def swap(array, axes):
    return lax.all_to_all(array, axes, 0, 0, tiled=True)


CHUNKS = 2


def body(q_raw, k_raw, values, grad_out, q_gain, k_gain, patch_counts, assignment, loader_shard):
    width = q_raw.shape[1]
    cycle, outer, inner = (lax.axis_size(name) for name in ("blk", "z", "yc"))
    q_gain_row, k_gain_row = q_gain.reshape(1, width), k_gain.reshape(1, width)
    tables = (x.reshape(-1, 128) for x in (patch_counts, assignment, loader_shard))
    packed, boundary = pack(
        q_raw, k_raw, values, grad_out, q_gain_row, k_gain_row, *tables, cycle, outer * inner, CHUNKS
    )
    arrived = [swap(x, "blk") for x in packed]
    results = [attention(boundary, x) for x in arrived]
    back = [swap(x, "blk") for x, _ in results]
    part = jnp.concatenate([p for _, p in results], axis=0)
    count = part.size
    part = part.reshape(1, count // 128, 128)
    part = swap(jnp.broadcast_to(part, (inner,) + part.shape[1:]), "yc")
    part = jnp.sum(part, axis=0, keepdims=True)
    part = swap(jnp.broadcast_to(part, (outer * cycle,) + part.shape[1:]), ("z", "blk"))
    part = jnp.sum(part.reshape(outer, cycle, -1, 2, 128), axis=0)
    q_gain_grad = part[:, :, 0].reshape(width) / q_gain
    k_gain_grad = part[:, :, 1].reshape(width) / k_gain
    return (*finish(back, q_raw, k_raw, q_gain_row, k_gain_row), q_gain_grad, k_gain_grad)


def solution(mesh):
    groups = mesh.shape["dp"]
    inner = min(16, groups)
    split = Mesh(
        mesh.devices.reshape(mesh.shape["blk"], groups // inner, inner), ("blk", "z", "yc")
    )
    rows = P(("z", "yc", "blk"), None)
    return jax.shard_map(
        body,
        mesh=split,
        in_specs=(rows,) * 4 + (P(),) * 5,
        out_specs=(rows,) * 4 + (P(),) * 2,
        check_vma=False,
    )
```

time: 299 us -> 126 us (0.42)
  waiting for transfers between devices: 112 us -> 16.7 us
  blocking collectives: 118 us -> 76.4 us
  matrix products: 30.5 us -> 0 us
  between operations: 14.7 us -> 0.72 us
  Pallas kernels: 0 us -> 13 us
  other arithmetic: 11.1 us -> 1.29 us
  starting transfers between devices: 0.16 us -> 7.16 us
  local copies, waits for them, and re-layouts: 11.8 us -> 8.61 us
    all_gather x4 -> x0, waiting for transfers between devices: 111 us -> none  [the longest x1 38.9 us: body(): lax.all_gather(key_normed, 'blk', axis=0, tiled=True)]
    psum x1 -> x0, blocking collectives: 98.9 us -> none  [body(): q_gain_grad, k_gain_grad = lax.psum((q_part, k_part), ('blk', 'dp'))]
    all_to_all x0 -> x4, blocking collectives: none -> 76.4 us  [swap(): return lax.all_to_all(array, axes, 0, 0, tiled=True)]
    dot_general x7 -> x0, matrix products: 30.5 us -> none  [the longest x1 6.38 us: forward_rows(): jnp.einsum('qhk,khd->qhd', weighted_half, key_all, preferred_element_type...]
    all_gather x2 -> x0, blocking collectives: 19.3 us -> none  [the longest x1 9.78 us: body(): lax.all_gather(row_delta, 'blk', axis=0, tiled=True)]
    all_to_all x0 -> x2, waiting for transfers between devices: none -> 16.7 us  [swap(): return lax.all_to_all(array, axes, 0, 0, tiled=True)]
    pallas_call x0 -> x4, Pallas kernels: none -> 13 us  [the longest x2 7.95 us: attention(): pl.pallas_call(attention_kernel, grid=(heads,), in_specs=[pl.BlockSpec(me...]
    all_to_all x0 -> x2, starting transfers between devices: none -> 7.16 us  [swap(): return lax.all_to_all(array, axes, 0, 0, tiled=True)]
  transfers between devices with their start and end apart: 4 -> 2, of which waited for: 3 -> 2; matrix products, arithmetic and copies ran while one was open for 14% -> 1% of each run, Pallas kernels for 0% -> 3%
where the time goes in v1:
time: 126 us; the launch traced here: 124 us
  blocking collectives  76.4 us (61%)
  waiting for transfers between devices  16.7 us (13%)
  Pallas kernels  13 us (10%)
  local copies, waits for them, and re-layouts  8.61 us (7%)
  starting transfers between devices  7.16 us (6%)
  other arithmetic  1.29 us (1%)
    all_to_all x4, blocking collectives, swap(): return lax.all_to_all(array, axes, 0, 0, tiled=True)  76.4 us
    all_to_all x2, waiting for transfers between devices, swap(): return lax.all_to_all(array, axes, 0, 0, tiled=True)  16.7 us
    unnamed x26, local copies, waits for them, and re-layouts  8.57 us
    pallas_call x2, Pallas kernels, attention(): pl.pallas_call(attention_kernel, grid=(heads,), in_specs=[pl.BlockSpec(me...  7.95 us
    all_to_all x2, starting transfers between devices, swap(): return lax.all_to_all(array, axes, 0, 0, tiled=True)  7.16 us
    pallas_call x1, Pallas kernels, pack(): pl.pallas_call(functools.partial(pack_kernel, group_count, cycle, chunks)...  2.64 us
  transfers between devices with their start and end apart: 2, of which 2 were waited for; matrix products, arithmetic and copies ran while one was open for 1% of the time, Pallas kernels for 3%

profile of v1, /device:TPU:1, one launch (start us, length us, event | category | flops | bytes accessed | tf_op | source)
XLA Modules:
  0.0 123.9 jit_solution(9078940921189643985)
XLA Ops:
  0.6 0.7 copy-done.7
  1.3 1.0 copy-done
  2.4 1.0 copy-done.2
  3.4 1.0 copy-done.5
  4.5 1.0 copy-done.6
  5.5 0.7 copy-done.8
  6.2 0.7 copy-done.10
  6.9 0.7 copy-done.11
  7.6 0.7 copy-done.12
  8.2 2.6 %pack.1 = (bf16[4,4,128,256]{3,2,1,0:T(8,128)(2,1)S(1)}, bf16[4,4,128,256]{3,2,1,0:T(8,128)(2,1)}, s32[1]{0:T(128)}) custom-call(s32[4,128]{1,0:T(4,128)S(1)} %bitcast.13, s32[4,128]{1,0:T(4,128)S(1)} %bitcast.14, s32[4,128]{1,0:T(4,128)S(1)} %bitcast.15, bf16[128,2048]{1,0:T(8,128)(2,1)S(1)} %copy-done, bf16[128,2048]{1,0:T(8,128)(2,1)S(1)} %copy-done.2, ...), custom_call_target="tpu_custom_call" | custom-call | flops 3145728 | bytes 4194304 | tf_op jit(solution)/shard_map/pack/pallas_call | solution.py:85
  10.9 15.1 %all_to_all.30.x_ref = bf16[4,4,128,256]{3,2,1,0:T(8,128)(2,1)S(1)} all-to-all(bf16[4,4,128,256]{3,2,1,0:T(8,128)(2,1)S(1)} %get-tuple-element.18), channel_id=1, replica_groups=mesh['blk'=4,'z'=8,'yc'=16] {'blk'}, dimensions={0} | all-to-all | bytes 2097152 | tf_op jit(solution)/shard_map/all_to_all | solution.py:199
  26.0 3.5 %all-to-all-start.2 = ((bf16[4,4,128,256]{3,2,1,0:T(8,128)(2,1)}), bf16[4,4,128,256]{3,2,1,0:T(8,128)(2,1)S(1)}, u32[]{:S(2)}, u32[]{:S(2)}) async-start(bf16[4,4,128,256]{3,2,1,0:T(8,128)(2,1)} %get-tuple-element.20), calls=%async_computation.2 | async-start | bytes 2097152 | tf_op jit(solution)/shard_map/all_to_all | solution.py:199
  29.5 4.0 %attention.2 = (bf16[4,4,128,256]{3,2,1,0:T(8,128)(2,1)S(1)}, f32[2,2,128]{2,1,0:T(2,128)S(1)}) custom-call(s32[1]{0:T(128)} %get-tuple-element.17.boundary_ref, bf16[4,4,128,256]{3,2,1,0:T(8,128)(2,1)S(1)} %all_to_all.30.x_ref), custom_call_target="tpu_custom_call" | custom-call | flops 939524096 | bytes 4194304 | tf_op jit(solution)/shard_map/attention/pallas_call | solution.py:143
  33.5 5.7 %all-to-all-done.2.x_ref = bf16[4,4,128,256]{3,2,1,0:T(8,128)(2,1)S(1)} async-done(((bf16[4,4,128,256]{3,2,1,0:T(8,128)(2,1)}), bf16[4,4,128,256]{3,2,1,0:T(8,128)(2,1)S(1)}, u32[]{:S(2)}, u32[]{:S(2)}) %all-to-all-start.2) | async-done | bytes 1048608 | tf_op jit(solution)/shard_map/all_to_all | solution.py:199
  39.2 4.0 %attention.3 = (bf16[4,4,128,256]{3,2,1,0:T(8,128)(2,1)S(1)}, f32[2,2,128]{2,1,0:T(2,128)S(1)}) custom-call(s32[1]{0:T(128)} %get-tuple-element.17.boundary_ref, bf16[4,4,128,256]{3,2,1,0:T(8,128)(2,1)S(1)} %all-to-all-done.2.x_ref), custom_call_target="tpu_custom_call" | custom-call | flops 939524096 | bytes 4194304 | tf_op jit(solution)/shard_map/attention/pallas_call | solution.py:143
  43.2 1.0 copy-done.4
  44.2 24.7 %all_to_all.31 = f32[16,8,128]{2,1,0:T(8,128)S(1)} all-to-all(f32[16,8,128]{2,1,0:T(8,128)S(1)} %broadcast_in_dim.14), channel_id=1, replica_groups=mesh['blk'=4,'z'=8,'yc'=16] {'yc'}, dimensions={0} | all-to-all | bytes 131072 | tf_op jit(solution)/shard_map/all_to_all | solution.py:199
  69.0 20.6 %all_to_all.32 = f32[32,8,128]{2,1,0:T(8,128)S(1)} all-to-all(f32[32,8,128]{2,1,0:T(8,128)S(1)} %broadcast_in_dim.15), channel_id=1, replica_groups=mesh['blk'=4,'z'=8,'yc'=16] {'z','blk'}, dimensions={0} | all-to-all | bytes 262144 | tf_op jit(solution)/shard_map/all_to_all | solution.py:199
  89.6 15.9 %all_to_all.33.refs_0_ = bf16[4,4,128,256]{3,2,1,0:T(8,128)(2,1)S(1)} all-to-all(bf16[4,4,128,256]{3,2,1,0:T(8,128)(2,1)S(1)} %get-tuple-element.19), channel_id=1, replica_groups=mesh['blk'=4,'z'=8,'yc'=16] {'blk'}, dimensions={0} | all-to-all | bytes 2097152 | tf_op jit(solution)/shard_map/all_to_all | solution.py:199
  105.6 3.6 %all-to-all-start.3 = ((bf16[4,4,128,256]{3,2,1,0:T(8,128)(2,1)}), bf16[4,4,128,256]{3,2,1,0:T(8,128)(2,1)S(1)}, u32[]{:S(2)}, u32[]{:S(2)}) async-start(bf16[4,4,128,256]{3,2,1,0:T(8,128)(2,1)} %copy-done.4), calls=%async_computation.3 | async-start | bytes 2097152 | tf_op jit(solution)/shard_map/all_to_all | solution.py:199
  109.3 0.6 div.7
  109.9 0.6 div.6
  110.5 11.0 %all-to-all-done.3.refs_1_ = bf16[4,4,128,256]{3,2,1,0:T(8,128)(2,1)S(1)} async-done(((bf16[4,4,128,256]{3,2,1,0:T(8,128)(2,1)}), bf16[4,4,128,256]{3,2,1,0:T(8,128)(2,1)S(1)}, u32[]{:S(2)}, u32[]{:S(2)}) %all-to-all-start.3) | async-done | bytes 1048608 | tf_op jit(solution)/shard_map/all_to_all | solution.py:199
  121.5 2.4 %finish.1 = (bf16[128,2048]{1,0:T(8,128)(2,1)}, bf16[128,2048]{1,0:T(8,128)(2,1)}, bf16[128,2048]{1,0:T(8,128)(2,1)}, bf16[128,2048]{1,0:T(8,128)(2,1)}) custom-call(bf16[4,4,128,256]{3,2,1,0:T(8,128)(2,1)S(1)} %all_to_all.33.refs_0_, bf16[4,4,128,256]{3,2,1,0:T(8,128)(2,1)S(1)} %all-to-all-done.3.refs_1_, bf16[128,2048]{1,0:T(8,128)(2,1)S(1)} %copy-done.1, ...), custom_call_target="tpu_custom_call" | custom-call | flops 5242880 | bytes 5242880 | tf_op jit(solution)/shard_map/finish/pallas_call | solution.py:185
  (22 shorter events, 0.1 us)
Async XLA Ops:
  0.6 0.7 copy-start.7
  1.3 1.0 copy-start
  2.4 1.0 copy-start.2
  3.4 1.0 copy-start.5
  4.5 1.0 copy-start.6
  5.5 0.7 copy-start.8
  6.2 0.7 copy-start.10
  6.9 0.7 copy-start.11
  7.6 0.7 copy-start.12
  26.0 13.2 %all-to-all-start.2 = ((bf16[4,4,128,256]{3,2,1,0:T(8,128)(2,1)}), bf16[4,4,128,256]{3,2,1,0:T(8,128)(2,1)S(1)}, u32[]{:S(2)}, u32[]{:S(2)}) async-start(bf16[4,4,128,256]{3,2,1,0:T(8,128)(2,1)} %get-tuple-element.20), calls=%async_computation.2 | async-start | bytes 2097152 | tf_op jit(solution)/shard_map/all_to_all | solution.py:199
  43.2 1.0 copy-start.4
  105.5 3.7 %copy-start.9 = (f32[2048]{0:T(1024)S(1)}, f32[2048]{0:T(1024)}, u32[]{:S(2)}) copy-start(f32[2048]{0:T(1024)} %param.14) | copy-start | bytes 24580
  105.5 15.9 %copy-start.1 = (bf16[128,2048]{1,0:T(8,128)(2,1)S(1)}, bf16[128,2048]{1,0:T(8,128)(2,1)}, u32[]{:S(2)}) copy-start(bf16[128,2048]{1,0:T(8,128)(2,1)} %refs_2_.1) | copy-start | bytes 1572868
  105.5 15.9 %copy-start.3 = (bf16[128,2048]{1,0:T(8,128)(2,1)S(1)}, bf16[128,2048]{1,0:T(8,128)(2,1)}, u32[]{:S(2)}) copy-start(bf16[128,2048]{1,0:T(8,128)(2,1)} %refs_3_.1) | copy-start | bytes 1572868
  105.6 15.9 %all-to-all-start.3 = ((bf16[4,4,128,256]{3,2,1,0:T(8,128)(2,1)}), bf16[4,4,128,256]{3,2,1,0:T(8,128)(2,1)S(1)}, u32[]{:S(2)}, u32[]{:S(2)}) async-start(bf16[4,4,128,256]{3,2,1,0:T(8,128)(2,1)} %copy-done.4), calls=%async_computation.3 | async-start | bytes 2097152 | tf_op jit(solution)/shard_map/all_to_all | solution.py:199

commit v2 on v1

v2 whole, which is shorter than its diff:
```python
import functools
import math

import jax
import jax.numpy as jnp
from jax import lax
from jax.experimental import pallas as pl
from jax.experimental.pallas import tpu as pltpu
from jax.sharding import Mesh, PartitionSpec as P

HEAD_DIM = 128
KINDS = 4
ROW_STEP = 64
HEAD_STEP = 2
KEY_STEP = 64
PART_ROWS = 32
GROUP_AXES = ("z", "y", "c")
MIB = 1024 * 1024

epsilon = 1e-06
masked_score = -1e30
log2_e = 1.4426950408889634


def whole_block(shape):
    return pl.BlockSpec(shape, lambda: (0,) * len(shape))


def sum_all(array):
    return jnp.sum(jnp.sum(array, axis=1, keepdims=True), axis=0, keepdims=True)


def group_table(counts, assignment, loader, group_index, group_count):
    shape = counts.shape
    entries = lax.broadcasted_iota(jnp.int32, shape, 0) * shape[1] + lax.broadcasted_iota(
        jnp.int32, shape, 1
    )
    living = counts > 0
    owned = living & (assignment == group_index)
    total = shape[0] * shape[1]
    first = jnp.where(owned, entries, total)
    first = jnp.min(jnp.min(first, axis=1, keepdims=True), axis=0, keepdims=True)
    last = jnp.where(owned, entries, -1)
    last = jnp.max(jnp.max(last, axis=1, keepdims=True), axis=0, keepdims=True)
    boundary = sum_all(jnp.where(entries == first, counts, 0))
    living_total = sum_all(living.astype(jnp.int32))

    def weight_of(entry):
        shard = sum_all(jnp.where(entries == entry, loader, 0))
        shared = sum_all((living & (loader == shard)).astype(jnp.int32))
        return living_total.astype(jnp.float32) / (group_count * shared).astype(jnp.float32)

    return boundary, weight_of(first), weight_of(last)


def pack_kernel(group_count, cycle, *refs):
    small, large = refs[:5], refs[5:9]
    packed_ref, boundary_ref = refs[9:11]
    small_held = refs[11:16]
    large_held, packed_held, small_sems, large_sems, out_sems = refs[16:]
    rows, width = large[0].shape
    steps = rows // ROW_STEP
    heads = width // cycle // HEAD_DIM
    small_copies = [pltpu.make_async_copy(small[n], small_held[n], small_sems.at[n]) for n in range(5)]
    for copy in small_copies:
        copy.start()

    def large_copy(n, step):
        block = pl.ds(step * ROW_STEP, ROW_STEP)
        return pltpu.make_async_copy(large[n].at[block], large_held.at[n, block], large_sems.at[n, step])

    def out_copy(d, step):
        block = pl.ds(step * ROW_STEP, ROW_STEP)
        return pltpu.make_async_copy(
            packed_held.at[d, :, :, block], packed_ref.at[d, :, :, block], out_sems.at[d, step]
        )

    for step in range(steps):
        for n in range(KINDS):
            large_copy(n, step).start()
    for copy in small_copies:
        copy.wait()
    boundary, weight_first, weight_last = group_table(
        small_held[0][...], small_held[1][...], small_held[2][...], lax.axis_index(GROUP_AXES), group_count
    )
    boundary_ref[...] = jnp.broadcast_to(boundary, boundary_ref.shape)
    for step in range(steps):
        block = slice(step * ROW_STEP, (step + 1) * ROW_STEP)
        position = (
            lax.axis_index("blk") * rows + step * ROW_STEP
            + lax.broadcasted_iota(jnp.int32, (ROW_STEP, 1), 0)
        )
        row_weight = jnp.where(position < boundary, weight_first, weight_last)
        for n in range(KINDS):
            large_copy(n, step).wait()
            array = large_held[n, block]
            if n < 2:
                widened = array.astype(jnp.float32)
                inverse = lax.rsqrt(jnp.mean(widened * widened, axis=-1, keepdims=True) + epsilon)
                array = (widened * inverse * small_held[3 + n][...]).astype(jnp.bfloat16)
            if n == 3:
                array = (array.astype(jnp.float32) * row_weight).astype(jnp.bfloat16)
            for d in range(cycle):
                for h in range(heads):
                    start = (d * heads + h) * HEAD_DIM
                    packed_held[d, h, n, block] = array[:, start : start + HEAD_DIM]
        for d in range(cycle):
            out_copy(d, step).start()
    for step in range(steps):
        for d in range(cycle):
            out_copy(d, step).wait()


def pack(q_raw, k_raw, values, grad_out, q_gain, k_gain, counts, assignment, loader, cycle, group_count):
    rows, width = q_raw.shape
    packed = jax.ShapeDtypeStruct((cycle, width // cycle // HEAD_DIM, KINDS, rows, HEAD_DIM), jnp.bfloat16)
    small = (counts, assignment, loader, q_gain, k_gain)
    return pl.pallas_call(
        functools.partial(pack_kernel, group_count, cycle),
        in_specs=[pl.BlockSpec(memory_space=pl.ANY)] * 9,
        out_specs=[pl.BlockSpec(memory_space=pl.ANY), pl.BlockSpec(memory_space=pltpu.VMEM)],
        out_shape=[packed, jax.ShapeDtypeStruct((8, 128), jnp.int32)],
        scratch_shapes=[pltpu.VMEM(x.shape, x.dtype) for x in small]
        + [
            pltpu.VMEM((KINDS, rows, width), jnp.bfloat16),
            pltpu.VMEM(packed.shape, packed.dtype),
            pltpu.SemaphoreType.DMA((5,)),
            pltpu.SemaphoreType.DMA((KINDS, rows // ROW_STEP)),
            pltpu.SemaphoreType.DMA((cycle, rows // ROW_STEP)),
        ],
        compiler_params=pltpu.CompilerParams(vmem_limit_bytes=60 * MIB),
        cost_estimate=pl.CostEstimate(flops=12 * rows * width, bytes_accessed=16 * rows * width, transcendentals=rows),
        name="pack",
    )(*small, q_raw, k_raw, values, grad_out)


def dot(a, b, a_dim, b_dim):
    return lax.dot_general(a, b, (((a_dim,), (b_dim,)), ((), ())), preferred_element_type=jnp.float32)


def fold(array, op):
    return op(array.reshape(-1, 8, array.shape[-1]), axis=0)


def attention_kernel(cycle, boundary_ref, x_ref, *rest):
    o_refs, part_ref = rest[:cycle], rest[cycle]
    side_ref, score_ref, grad_ref, softmax_ref, weighted_ref, score_grad_ref, held_ref = rest[cycle + 1 :]
    _, heads, kinds, rows, width = x_ref.shape
    slots = cycle * rows
    scale = HEAD_DIM ** (-0.5)
    boundary = boundary_ref[0:1, 0:1]
    step = pl.program_id(0)
    place = lax.axis_index("blk")
    key_steps = [slice(j, j + KEY_STEP) for j in range(0, slots, KEY_STEP)]
    query_side = (lax.broadcasted_iota(jnp.int32, (1, slots), 1) < boundary).astype(jnp.int32)

    @pl.when(step == 0)
    def _():
        side_ref[...] = (lax.broadcasted_iota(jnp.int32, side_ref.shape, 0) < boundary).astype(jnp.int32)

    def operands(h):
        return [x_ref[:, h, a].reshape(slots, width) for a in range(kinds)]

    def products(h):
        q, k, v, g = operands(h)
        scores = dot(k, q, 1, 1)
        top = None
        for down in key_steps:
            side = jnp.concatenate([side_ref[down]] * (slots // 128), axis=1)
            block = jnp.where(side == query_side, scores[down], masked_score)
            score_ref[h, down] = block
            block = fold(block, jnp.max)
            top = block if top is None else jnp.maximum(top, block)
        grad_ref[h] = dot(v, g, 1, 1)
        return jnp.max(top, axis=0, keepdims=True)

    def weights(h, top):
        total = 0.0
        for down in key_steps:
            block = jnp.exp2((score_ref[h, down] - top) * (scale * log2_e))
            score_ref[h, down] = block
            total += fold(block, jnp.sum)
        inverse = 1.0 / jnp.sum(total, axis=0, keepdims=True)
        row_delta = 0.0
        for down in key_steps:
            softmax = score_ref[h, down] * inverse
            weighted = softmax * grad_ref[h, down]
            row_delta += fold(weighted, jnp.sum)
            softmax_ref[h, down] = softmax.astype(jnp.bfloat16)
            weighted_ref[h, down] = weighted.astype(jnp.bfloat16)
        row_delta = jnp.sum(row_delta, axis=0, keepdims=True)
        for down in key_steps:
            softmax = score_ref[h, down] * inverse
            score_grad_ref[h, down] = (softmax * (grad_ref[h, down] - row_delta)).astype(jnp.bfloat16)
        return row_delta

    def results(h, row_delta):
        q, k, v, g = operands(h)
        both = dot(jnp.concatenate([v, k], axis=1), softmax_ref[h], 0, 0)
        query_grad = (scale * (dot(k, weighted_ref[h], 0, 0) - row_delta * both[width:])).T
        key_grad = scale * dot(score_grad_ref[h], q, 1, 0)
        held_ref[h, 0] = both[:width].T.astype(jnp.bfloat16)
        held_ref[h, 1] = query_grad.astype(jnp.bfloat16)
        held_ref[h, 2] = key_grad.astype(jnp.bfloat16)
        held_ref[h, 3] = dot(softmax_ref[h], g, 1, 0).astype(jnp.bfloat16)
        for s in range(cycle):
            first = pl.multiple_of(lax.rem(place + cycle - s, cycle) * rows, rows)
            o_refs[s][h] = held_ref[h, :, pl.ds(first, rows), :]
        query_part = jnp.sum(query_grad * q.astype(jnp.float32), axis=0, keepdims=True)
        key_part = jnp.sum(key_grad * k.astype(jnp.float32), axis=0, keepdims=True)
        parts = jnp.concatenate([query_part, key_part], axis=0)
        at = pl.ds(2 * (step * heads + h), 2)
        part_ref[:, at, :] = jnp.broadcast_to(parts, (part_ref.shape[0], 2, width))

    top = products(0)
    for h in range(heads):
        row_delta = weights(h, top)
        if h + 1 < heads:
            top = products(h + 1)
        results(h, row_delta)


def attention(boundary, arrived, copies):
    cycle, heads, kinds, rows, width = arrived.shape
    slots = cycle * rows
    parts = (copies, PART_ROWS, width)
    square = (HEAD_STEP, slots, slots)
    out = pl.pallas_call(
        functools.partial(attention_kernel, cycle),
        grid=(heads // HEAD_STEP,),
        in_specs=[
            pl.BlockSpec(boundary.shape, lambda h: (0, 0)),
            pl.BlockSpec((cycle, HEAD_STEP, kinds, rows, width), lambda h: (0, h, 0, 0, 0)),
        ],
        out_specs=[pl.BlockSpec((HEAD_STEP, kinds, rows, width), lambda h: (h, 0, 0, 0))] * cycle
        + [pl.BlockSpec(parts, lambda h: (0, 0, 0))],
        out_shape=[jax.ShapeDtypeStruct((heads, kinds, rows, width), jnp.bfloat16)] * cycle
        + [jax.ShapeDtypeStruct(parts, jnp.float32)],
        scratch_shapes=[
            pltpu.VMEM((slots, 128), jnp.int32),
            pltpu.VMEM(square, jnp.float32),
            pltpu.VMEM(square, jnp.float32),
            pltpu.VMEM(square, jnp.bfloat16),
            pltpu.VMEM(square, jnp.bfloat16),
            pltpu.VMEM(square, jnp.bfloat16),
            pltpu.VMEM((HEAD_STEP, kinds, slots, width), jnp.bfloat16),
        ],
        compiler_params=pltpu.CompilerParams(vmem_limit_bytes=32 * MIB),
        cost_estimate=pl.CostEstimate(
            flops=14 * heads * slots * slots * width, bytes_accessed=16 * slots * width * heads,
            transcendentals=heads * slots * slots,
        ),
        name="attention",
    )(boundary, arrived)
    return out[:cycle], out[cycle]


def finish_kernel(cycle, *refs):
    back_refs, raws, gains = refs[:cycle], refs[cycle : cycle + 2], refs[cycle + 2 : cycle + 4]
    att_ref, dq_ref, dk_ref, dv_ref = refs[cycle + 4 : cycle + 8]
    raw_held, grad_held, raw_sems, grad_sems, copy_sems = refs[cycle + 8 :]
    heads, kinds, rows, _ = back_refs[0].shape
    share = heads * HEAD_DIM
    width = share * cycle
    steps = rows // ROW_STEP
    place = lax.axis_index("blk")
    starts = [pl.multiple_of(lax.rem(place + s, cycle) * share, share) for s in range(cycle)]

    def raw_copy(n, step):
        block = pl.ds(step * ROW_STEP, ROW_STEP)
        return pltpu.make_async_copy(raws[n].at[block], raw_held.at[n, block], raw_sems.at[n, step])

    def grad_copy(n, step):
        block = pl.ds(step * ROW_STEP, ROW_STEP)
        return pltpu.make_async_copy(
            grad_held.at[n, block], (dq_ref, dk_ref)[n].at[block], grad_sems.at[n, step]
        )

    def plain_copy(n, s, h):
        target = (att_ref, dv_ref)[n].at[:, pl.ds(starts[s] + h * HEAD_DIM, HEAD_DIM)]
        return pltpu.make_async_copy(back_refs[s].at[h, 3 * n], target, copy_sems.at[n, s, h])

    plain = [plain_copy(n, s, h) for n in range(2) for s in range(cycle) for h in range(heads)]
    for step in range(steps):
        for n in range(2):
            raw_copy(n, step).start()
    for copy in plain:
        copy.start()
    for step in range(steps):
        block = slice(step * ROW_STEP, (step + 1) * ROW_STEP)
        for n in range(2):
            raw_copy(n, step).wait()
            raw = [raw_held[n, block, pl.ds(start, share)].astype(jnp.float32) for start in starts]
            grad = [
                jnp.concatenate([back[h, 1 + n, block] for h in range(heads)], axis=1).astype(jnp.float32)
                * gains[n][:, pl.ds(start, share)]
                for back, start in zip(back_refs, starts)
            ]
            square = sum(jnp.sum(x * x, axis=-1, keepdims=True) for x in raw)
            along = sum(jnp.sum(x * y, axis=-1, keepdims=True) for x, y in zip(raw, grad))
            inverse = lax.rsqrt(square / width + epsilon)
            along = along * inverse * inverse / width
            for x, y, start in zip(raw, grad, starts):
                grad_held[n, block, pl.ds(start, share)] = (inverse * (y - x * along)).astype(jnp.bfloat16)
            grad_copy(n, step).start()
    for copy in plain:
        copy.wait()
    for step in range(steps):
        for n in range(2):
            grad_copy(n, step).wait()


def finish(back, q_raw, k_raw, q_gain, k_gain):
    rows, width = q_raw.shape
    cycle = len(back)
    heads = back[0].shape[0]
    steps = rows // ROW_STEP
    return pl.pallas_call(
        functools.partial(finish_kernel, cycle),
        in_specs=[whole_block(back[0].shape)] * cycle
        + [pl.BlockSpec(memory_space=pl.ANY)] * 2
        + [whole_block((1, width))] * 2,
        out_specs=[pl.BlockSpec(memory_space=pl.ANY)] * 4,
        out_shape=[jax.ShapeDtypeStruct((rows, width), jnp.bfloat16)] * 4,
        scratch_shapes=[
            pltpu.VMEM((2, rows, width), jnp.bfloat16),
            pltpu.VMEM((2, rows, width), jnp.bfloat16),
            pltpu.SemaphoreType.DMA((2, steps)),
            pltpu.SemaphoreType.DMA((2, steps)),
            pltpu.SemaphoreType.DMA((2, cycle, heads)),
        ],
        compiler_params=pltpu.CompilerParams(vmem_limit_bytes=32 * MIB),
        cost_estimate=pl.CostEstimate(flops=20 * rows * width, bytes_accessed=20 * rows * width, transcendentals=rows),
        name="finish",
    )(*back, q_raw, k_raw, q_gain, k_gain)


def respread_kernel(part_ref, o_ref):
    o_ref[...] = jnp.broadcast_to(jnp.sum(part_ref[...], axis=0, keepdims=True), o_ref.shape)


def respread(part, copies):
    out_shape = (copies,) + part.shape[1:]
    return pl.pallas_call(
        respread_kernel,
        in_specs=[whole_block(part.shape)],
        out_specs=whole_block(out_shape),
        out_shape=jax.ShapeDtypeStruct(out_shape, jnp.float32),
        compiler_params=pltpu.CompilerParams(vmem_limit_bytes=32 * MIB),
        name="respread",
    )(part)


def gain_grad_kernel(part_ref, q_gain_ref, k_gain_ref, q_ref, k_ref):
    cycle, count, _ = part_ref.shape
    for n, (gain_ref, out_ref) in enumerate(((q_gain_ref, q_ref), (k_gain_ref, k_ref))):
        rows = jnp.concatenate(
            [part_ref[d, 2 * h + n : 2 * h + n + 1] for d in range(cycle) for h in range(count // 2)], axis=0
        )
        out_ref[...] = rows / gain_ref[...]


def gain_grad(part, q_gain, k_gain):
    shape = (q_gain.size // 128, 128)
    out = pl.pallas_call(
        gain_grad_kernel,
        in_specs=[whole_block(part.shape)] + [whole_block(shape)] * 2,
        out_specs=[whole_block(shape)] * 2,
        out_shape=[jax.ShapeDtypeStruct(shape, jnp.float32)] * 2,
        compiler_params=pltpu.CompilerParams(vmem_limit_bytes=32 * MIB),
        name="gain_grad",
    )(part, q_gain.reshape(shape), k_gain.reshape(shape))
    return [x.reshape(-1) for x in out]


def swap(array, axes):
    return lax.all_to_all(array, axes, 0, 0, tiled=True)


def body(q_raw, k_raw, values, grad_out, q_gain, k_gain, patch_counts, assignment, loader_shard):
    width = q_raw.shape[1]
    cycle, outer, inner, cores = (lax.axis_size(name) for name in ("blk", *GROUP_AXES))
    q_gain_row, k_gain_row = q_gain.reshape(1, width), k_gain.reshape(1, width)
    tables = (x.reshape(-1, 128) for x in (patch_counts, assignment, loader_shard))
    packed, boundary = pack(
        q_raw, k_raw, values, grad_out, q_gain_row, k_gain_row, *tables, cycle, outer * inner * cores
    )
    slots, part = attention(boundary, swap(packed, "blk"), inner * cores)
    back = [slots[0]] + [
        lax.ppermute(slots[s], "blk", [(i, (i - s) % cycle) for i in range(cycle)]) for s in range(1, cycle)
    ]

    part = respread(swap(part, ("y", "c"))[:, : 2 * slots[0].shape[0]], outer)
    part = respread(swap(part, "z"), cycle)
    part = swap(part, "blk")
    return (*finish(back, q_raw, k_raw, q_gain_row, k_gain_row), *gain_grad(part, q_gain, k_gain))


def solution(mesh):
    groups = mesh.shape["dp"]
    cores = math.gcd(groups, 2)
    inner = math.gcd(groups // cores, 8)
    split = Mesh(
        mesh.devices.reshape(mesh.shape["blk"], groups // cores // inner, inner, cores), ("blk", *GROUP_AXES)
    )
    rows = P((*GROUP_AXES, "blk"), None)
    return jax.shard_map(
        body,
        mesh=split,
        in_specs=(rows,) * 4 + (P(),) * 5,
        out_specs=(rows,) * 4 + (P(),) * 2,
        check_vma=False,
    )
```

time: 126 us -> 89.5 us (0.71); the launches traced: 124 us -> 89 us
  blocking collectives: 76.4 us -> 42 us
  starting transfers between devices: 7.16 us -> 25 us
  waiting for transfers between devices: 16.7 us -> 5.83 us
  local copies, waits for them, and re-layouts: 8.61 us -> 1.62 us
  other arithmetic: 1.29 us -> 0 us
    all_to_all x4 -> x2, blocking collectives: 76.4 us -> 42 us  [swap(): return lax.all_to_all(array, axes, 0, 0, tiled=True)]
    all_to_all x2, waiting for transfers between devices: 16.7 us -> 5.82 us  [swap(): return lax.all_to_all(array, axes, 0, 0, tiled=True)]
    all_to_all x2, starting transfers between devices: 7.16 us -> 17.2 us  [swap(): return lax.all_to_all(array, axes, 0, 0, tiled=True)]
    ppermute x0 -> x3, starting transfers between devices: none -> 7.8 us  [body(): lax.ppermute(slots[s], 'blk', [(i, (i - s) % cycle) for i in range(cycle)])]
    unnamed x26 -> x16, local copies, waits for them, and re-layouts: 8.57 us -> 1.61 us
    pallas_call x4 -> x6, Pallas kernels: 13 us -> 13.8 us  [the longest x1 6.13 us: attention(): pl.pallas_call(functools.partial(attention_kernel, cycle), grid=(heads //...]
  transfers between devices with their start and end apart: 2 -> 5, of which waited for: 2 -> 2; matrix products, arithmetic and copies ran while one was open for 1% -> 0% of each run, Pallas kernels for 3% -> 3%
where the time goes in v2:
time: 89.5 us; the launch traced here: 89 us
  blocking collectives  42 us (47%)
  starting transfers between devices  25 us (28%)
  Pallas kernels  13.8 us (15%)
  waiting for transfers between devices  5.83 us (7%)
  local copies, waits for them, and re-layouts  1.62 us (2%)
    all_to_all x2, blocking collectives, swap(): return lax.all_to_all(array, axes, 0, 0, tiled=True)  42 us
    all_to_all x2, starting transfers between devices, swap(): return lax.all_to_all(array, axes, 0, 0, tiled=True)  17.2 us
    ppermute x3, starting transfers between devices, body(): lax.ppermute(slots[s], 'blk', [(i, (i - s) % cycle) for i in range(cycle)])  7.8 us
    pallas_call x1, Pallas kernels, attention(): pl.pallas_call(functools.partial(attention_kernel, cycle), grid=(heads //...  6.13 us
    all_to_all x2, waiting for transfers between devices, swap(): return lax.all_to_all(array, axes, 0, 0, tiled=True)  5.82 us
    pallas_call x1, Pallas kernels, pack(): pl.pallas_call(functools.partial(pack_kernel, group_count, cycle), in_spe...  4.27 us
    pallas_call x1, Pallas kernels, finish(): pl.pallas_call(functools.partial(finish_kernel, cycle), in_specs=[whole_b...  2.15 us
  transfers between devices with their start and end apart: 5, of which 2 were waited for; matrix products, arithmetic and copies ran while one was open for 0% of the time, Pallas kernels for 3%

profile of v2, /device:TPU:1, one launch (start us, length us, event | category | flops | bytes accessed | tf_op | source)
XLA Modules:
  0.0 89.0 jit_solution(440505651121881221)
XLA Ops:
  0.6 4.3 %pack.1 = (bf16[4,4,4,128,128]{4,3,2,1,0:T(8,128)(2,1)}, s32[8,128]{1,0:T(8,128)}) custom-call(s32[4,128]{1,0:T(4,128)} %bitcast.15, s32[4,128]{1,0:T(4,128)} %bitcast.16, s32[4,128]{1,0:T(4,128)} %bitcast.17, f32[1,2048]{1,0:T(1,128)} %bitcast.9, f32[1,2048]{1,0:T(1,128)} %bitcast.12, bf16[128,2048]{1,0:T(8,128)(2,1)} %refs_4_.1, ...), custom_call_target="tpu_custom_call" | custom-call | flops 3145728 | bytes 4194304 | tf_op jit(solution)/shard_map/pack/pallas_call | solution.py:118
  4.9 0.0 copy-start.7
  4.9 25.3 %all_to_all.20.x_ref = bf16[4,4,4,128,128]{4,3,2,1,0:T(8,128)(2,1)S(1)} all-to-all(bf16[4,4,4,128,128]{4,3,2,1,0:T(8,128)(2,1)} %get-tuple-element.20), channel_id=1, replica_groups=mesh['blk'=4,'z'=8,'y'=8,'c'=2] {'blk'}, dimensions={0} | all-to-all | bytes 4194304 | tf_op jit(solution)/shard_map/all_to_all | solution.py:377
  30.2 0.0 copy-done.7
  30.2 0.0 copy-start.3
  30.3 6.1 %attention.1 = (bf16[4,4,128,128]{3,2,1,0:T(8,128)(2,1)S(1)}, bf16[4,4,128,128]{3,2,1,0:T(8,128)(2,1)S(1)}, bf16[4,4,128,128]{3,2,1,0:T(8,128)(2,1)S(1)}, bf16[4...) custom-call(s32[8,128]{1,0:T(8,128)S(1)} %copy-done.7, bf16[4,4,4,128,128]{4,3,2,1,0:T(8,128)(2,1)S(1)} %all_to_all.20.x_ref), custom_call_target="tpu_custom_call" | custom-call | flops 1879048192 | bytes 4194304 | tf_op jit(solution)/shard_map/attention/pallas_call | solution.py:228
  36.4 0.8 copy-done.5
  37.2 0.8 copy-done.6
  38.0 13.9 %all-to-all-start.1 = ((f32[16,32,128]{2,1,0:T(8,128)}), f32[16,32,128]{2,1,0:T(8,128)S(1)}, u32[]{:S(2)}, u32[]{:S(2)}) async-start(f32[16,32,128]{2,1,0:T(8,128)} %get-tuple-element.29), calls=%async_computation.1 | async-start | bytes 524288 | tf_op jit(solution)/shard_map/all_to_all | solution.py:377
  51.9 2.8 %collective-permute-start = (bf16[4,4,128,128]{3,2,1,0:T(8,128)(2,1)}, bf16[4,4,128,128]{3,2,1,0:T(8,128)(2,1)S(1)}, u32[]{:S(2)}, u32[]{:S(2)}) collective-permute-start(bf16[4,4,128,128]{3,2,1,0:T(8,128)(2,1)} %copy-done.6), channel_id=1, source_target_pairs={{0,384},{128,0},{256,128},{384,256},{1,385},{129,1},{257,129},{385... | collective-permute-start | bytes 1572872 | tf_op jit(solution)/shard_map/ppermute | solution.py:390
  54.7 3.1 %collective-permute-start.1 = (bf16[4,4,128,128]{3,2,1,0:T(8,128)(2,1)}, bf16[4,4,128,128]{3,2,1,0:T(8,128)(2,1)S(1)}, u32[]{:S(2)}, u32[]{:S(2)}) collective-permute-start(bf16[4,4,128,128]{3,2,1,0:T(8,128)(2,1)} %copy-done.5), channel_id=1, source_target_pairs={{0,256},{128,384},{256,0},{384,128},{1,257},{129,385},{257,1},{385... | collective-permute-start | bytes 1572872 | tf_op jit(solution)/shard_map/ppermute | solution.py:390
  57.8 0.0 copy-done.4
  57.8 1.9 %collective-permute-start.2 = (bf16[4,4,128,128]{3,2,1,0:T(8,128)(2,1)}, bf16[4,4,128,128]{3,2,1,0:T(8,128)(2,1)S(1)}, u32[]{:S(2)}, u32[]{:S(2)}) collective-permute-start(bf16[4,4,128,128]{3,2,1,0:T(8,128)(2,1)} %copy-done.4), channel_id=1, source_target_pairs={{0,128},{128,256},{256,384},{384,0},{1,129},{129,257},{257,385},{3... | collective-permute-start | bytes 1572872 | tf_op jit(solution)/shard_map/ppermute | solution.py:390
  59.8 3.9 %all-to-all-done.1 = f32[16,32,128]{2,1,0:T(8,128)S(1)} async-done(((f32[16,32,128]{2,1,0:T(8,128)}), f32[16,32,128]{2,1,0:T(8,128)S(1)}, u32[]{:S(2)}, u32[]{:S(2)}) %all-to-all-start.1) | async-done | bytes 262176 | tf_op jit(solution)/shard_map/all_to_all | solution.py:377
  63.7 16.7 %all_to_all.21.part_ref = f32[8,8,128]{2,1,0:T(8,128)S(1)} all-to-all(f32[8,8,128]{2,1,0:T(8,128)S(1)} %respread.2), channel_id=1, replica_groups=mesh['blk'=4,'z'=8,'y'=8,'c'=2] {'z'}, dimensions={0} | all-to-all | bytes 65536 | tf_op jit(solution)/shard_map/all_to_all | solution.py:377
  80.4 0.6 respread.3
  81.0 3.2 %all-to-all-start.3 = ((f32[4,8,128]{2,1,0:T(8,128)}), f32[4,8,128]{2,1,0:T(8,128)S(1)}, u32[]{:S(2)}, u32[]{:S(2)}) async-start(f32[4,8,128]{2,1,0:T(8,128)} %respread.3), calls=%async_computation.3 | async-start | bytes 32768 | tf_op jit(solution)/shard_map/all_to_all | solution.py:377
  84.2 0.0 collective-permute-done.refs_1_
  84.2 0.0 collective-permute-done.1.refs_2_
  84.3 0.0 collective-permute-done.2.refs_3_
  84.3 0.0 copy-done
  84.3 2.1 %finish.1 = (bf16[128,2048]{1,0:T(8,128)(2,1)}, bf16[128,2048]{1,0:T(8,128)(2,1)}, bf16[128,2048]{1,0:T(8,128)(2,1)}, bf16[128,2048]{1,0:T(8,128)(2,1)}) custom-call(bf16[4,4,128,128]{3,2,1,0:T(8,128)(2,1)S(1)} %get-tuple-element.21.refs_0_, bf16[4,4,128,128]{3,2,1,0:T(8,128)(2,1)S(1)} %collective-permute-done.refs_1_, ...), custom_call_target="tpu_custom_call" | custom-call | flops 5242880 | bytes 5242880 | tf_op jit(solution)/shard_map/finish/pallas_call | solution.py:318
  86.5 2.0 %all-to-all-done.3.part_ref = f32[4,8,128]{2,1,0:T(8,128)S(1)} async-done(((f32[4,8,128]{2,1,0:T(8,128)}), f32[4,8,128]{2,1,0:T(8,128)S(1)}, u32[]{:S(2)}, u32[]{:S(2)}) %all-to-all-start.3) | async-done | bytes 16416 | tf_op jit(solution)/shard_map/all_to_all | solution.py:377
  88.4 0.6 gain_grad.1
  (11 shorter events, 0.0 us)
Async XLA Ops:
  4.9 25.3 %copy-start.7 = (s32[8,128]{1,0:T(8,128)S(1)}, s32[8,128]{1,0:T(8,128)}, u32[]{:S(2)}) copy-start(s32[8,128]{1,0:T(8,128)} %get-tuple-element.19.boundary_ref) | copy-start | bytes 12292
  30.2 54.0 %copy-start = (bf16[128,2048]{1,0:T(8,128)(2,1)S(1)}, bf16[128,2048]{1,0:T(8,128)(2,1)}, u32[]{:S(2)}) copy-start(bf16[128,2048]{1,0:T(8,128)(2,1)} %refs_4_.1) | copy-start | bytes 1572868
  30.2 54.0 %copy-start.1 = (bf16[128,2048]{1,0:T(8,128)(2,1)S(1)}, bf16[128,2048]{1,0:T(8,128)(2,1)}, u32[]{:S(2)}) copy-start(bf16[128,2048]{1,0:T(8,128)(2,1)} %refs_5_.3) | copy-start | bytes 1572868
  30.2 54.1 %copy-start.2 = (f32[2048]{0:T(1024)S(1)}, f32[2048]{0:T(1024)}, u32[]{:S(2)}) copy-start(f32[2048]{0:T(1024)} %param.13) | copy-start | bytes 24580
  30.2 54.1 %copy-start.3 = (f32[2048]{0:T(1024)S(1)}, f32[2048]{0:T(1024)}, u32[]{:S(2)}) copy-start(f32[2048]{0:T(1024)} %param.14) | copy-start | bytes 24580
  36.4 0.8 copy-start.5
  37.2 0.8 copy-start.6
  38.0 19.8 %copy-start.4 = (bf16[4,4,128,128]{3,2,1,0:T(8,128)(2,1)}, bf16[4,4,128,128]{3,2,1,0:T(8,128)(2,1)S(1)}, u32[]{:S(2)}) copy-start(bf16[4,4,128,128]{3,2,1,0:T(8,128)(2,1)S(1)} %get-tuple-element.24) | copy-start | bytes 1572868
  38.0 25.6 %all-to-all-start.1 = ((f32[16,32,128]{2,1,0:T(8,128)}), f32[16,32,128]{2,1,0:T(8,128)S(1)}, u32[]{:S(2)}, u32[]{:S(2)}) async-start(f32[16,32,128]{2,1,0:T(8,128)} %get-tuple-element.29), calls=%async_computation.1 | async-start | bytes 524288 | tf_op jit(solution)/shard_map/all_to_all | solution.py:377
  51.9 32.3 %collective-permute-start = (bf16[4,4,128,128]{3,2,1,0:T(8,128)(2,1)}, bf16[4,4,128,128]{3,2,1,0:T(8,128)(2,1)S(1)}, u32[]{:S(2)}, u32[]{:S(2)}) collective-permute-start(bf16[4,4,128,128]{3,2,1,0:T(8,128)(2,1)} %copy-done.6), channel_id=1, source_target_pairs={{0,384},{128,0},{256,128},{384,256},{1,385},{129,1},{257,129},{385... | collective-permute-start | bytes 1572872 | tf_op jit(solution)/shard_map/ppermute | solution.py:390
  54.7 29.5 %collective-permute-start.1 = (bf16[4,4,128,128]{3,2,1,0:T(8,128)(2,1)}, bf16[4,4,128,128]{3,2,1,0:T(8,128)(2,1)S(1)}, u32[]{:S(2)}, u32[]{:S(2)}) collective-permute-start(bf16[4,4,128,128]{3,2,1,0:T(8,128)(2,1)} %copy-done.5), channel_id=1, source_target_pairs={{0,256},{128,384},{256,0},{384,128},{1,257},{129,385},{257,1},{385... | collective-permute-start | bytes 1572872 | tf_op jit(solution)/shard_map/ppermute | solution.py:390
  57.8 26.4 %collective-permute-start.2 = (bf16[4,4,128,128]{3,2,1,0:T(8,128)(2,1)}, bf16[4,4,128,128]{3,2,1,0:T(8,128)(2,1)S(1)}, u32[]{:S(2)}, u32[]{:S(2)}) collective-permute-start(bf16[4,4,128,128]{3,2,1,0:T(8,128)(2,1)} %copy-done.4), channel_id=1, source_target_pairs={{0,128},{128,256},{256,384},{384,0},{1,129},{129,257},{257,385},{3... | collective-permute-start | bytes 1572872 | tf_op jit(solution)/shard_map/ppermute | solution.py:390
  81.0 7.4 %all-to-all-start.3 = ((f32[4,8,128]{2,1,0:T(8,128)}), f32[4,8,128]{2,1,0:T(8,128)S(1)}, u32[]{:S(2)}, u32[]{:S(2)}) async-start(f32[4,8,128]{2,1,0:T(8,128)} %respread.3), calls=%async_computation.3 | async-start | bytes 32768 | tf_op jit(solution)/shard_map/all_to_all | solution.py:377

commit v3 on v2

--- a/solution.py
+++ b/solution.py
@@ -10,6 +10,7 @@
 
 HEAD_DIM = 128
 KINDS = 4
+PACK_STEP = 128
 ROW_STEP = 64
 HEAD_STEP = 2
 KEY_STEP = 64
@@ -23,7 +24,7 @@
 
 
 def whole_block(shape):
-    return pl.BlockSpec(shape, lambda: (0,) * len(shape))
+    return pl.BlockSpec(memory_space=pltpu.VMEM)
 
 
 def sum_all(array):
@@ -57,41 +58,53 @@
     small, large = refs[:5], refs[5:9]
     packed_ref, boundary_ref = refs[9:11]
     small_held = refs[11:16]
-    large_held, packed_held, small_sems, large_sems, out_sems = refs[16:]
+    large_held, packed_held, boundary_held, small_sems, large_sems, out_sems, boundary_sem = refs[16:]
+    boundary_copy = pltpu.make_async_copy(boundary_held, boundary_ref, boundary_sem)
     rows, width = large[0].shape
-    steps = rows // ROW_STEP
+    steps = rows // PACK_STEP
     heads = width // cycle // HEAD_DIM
     small_copies = [pltpu.make_async_copy(small[n], small_held[n], small_sems.at[n]) for n in range(5)]
     for copy in small_copies:
         copy.start()
 
     def large_copy(n, step):
-        block = pl.ds(step * ROW_STEP, ROW_STEP)
+        block = pl.ds(step * PACK_STEP, PACK_STEP)
         return pltpu.make_async_copy(large[n].at[block], large_held.at[n, block], large_sems.at[n, step])
 
-    def out_copy(d, step):
-        block = pl.ds(step * ROW_STEP, ROW_STEP)
-        return pltpu.make_async_copy(
-            packed_held.at[d, :, :, block], packed_ref.at[d, :, :, block], out_sems.at[d, step]
-        )
-
-    for step in range(steps):
-        for n in range(KINDS):
+    def out_copies(n):
+        if n == 2:
+            return [
+                pltpu.make_async_copy(
+                    large_held.at[2, :, pl.ds((d * heads + h) * HEAD_DIM, HEAD_DIM)],
+                    packed_ref.at[d, h, 2],
+                    out_sems.at[d, KINDS + h],
+                )
+                for d in range(cycle)
+                for h in range(heads)
+            ]
+        return [
+            pltpu.make_async_copy(packed_held.at[d, :, n], packed_ref.at[d, :, n], out_sems.at[d, n])
+            for d in range(cycle)
+        ]
+
+    order = (2, 0, 1, 3)
+    for n in order:
+        for step in range(steps):
             large_copy(n, step).start()
-    for copy in small_copies:
-        copy.wait()
-    boundary, weight_first, weight_last = group_table(
-        small_held[0][...], small_held[1][...], small_held[2][...], lax.axis_index(GROUP_AXES), group_count
-    )
-    boundary_ref[...] = jnp.broadcast_to(boundary, boundary_ref.shape)
-    for step in range(steps):
-        block = slice(step * ROW_STEP, (step + 1) * ROW_STEP)
-        position = (
-            lax.axis_index("blk") * rows + step * ROW_STEP
-            + lax.broadcasted_iota(jnp.int32, (ROW_STEP, 1), 0)
-        )
-        row_weight = jnp.where(position < boundary, weight_first, weight_last)
-        for n in range(KINDS):
+    for n in order:
+        if n == 0:
+            for copy in small_copies[3:]:
+                copy.wait()
+        if n == 3:
+            for copy in small_copies[:3]:
+                copy.wait()
+            boundary, weight_first, weight_last = group_table(
+                small_held[0][...], small_held[1][...], small_held[2][...], lax.axis_index(GROUP_AXES), group_count
+            )
+            boundary_held[...] = jnp.broadcast_to(boundary, boundary_held.shape)
+            boundary_copy.start()
+        for step in range(steps):
+            block = slice(step * PACK_STEP, (step + 1) * PACK_STEP)
             large_copy(n, step).wait()
             array = large_held[n, block]
             if n < 2:
@@ -99,16 +112,24 @@
                 inverse = lax.rsqrt(jnp.mean(widened * widened, axis=-1, keepdims=True) + epsilon)
                 array = (widened * inverse * small_held[3 + n][...]).astype(jnp.bfloat16)
             if n == 3:
+                position = (
+                    lax.axis_index("blk") * rows + step * PACK_STEP
+                    + lax.broadcasted_iota(jnp.int32, (PACK_STEP, 1), 0)
+                )
+                row_weight = jnp.where(position < boundary, weight_first, weight_last)
                 array = (array.astype(jnp.float32) * row_weight).astype(jnp.bfloat16)
+            if n == 2:
+                continue
             for d in range(cycle):
                 for h in range(heads):
                     start = (d * heads + h) * HEAD_DIM
                     packed_held[d, h, n, block] = array[:, start : start + HEAD_DIM]
-        for d in range(cycle):
-            out_copy(d, step).start()
-    for step in range(steps):
-        for d in range(cycle):
-            out_copy(d, step).wait()
+        for copy in out_copies(n):
+            copy.start()
+    for n in order:
+        for copy in out_copies(n):
+            copy.wait()
+    boundary_copy.wait()
 
 
 def pack(q_raw, k_raw, values, grad_out, q_gain, k_gain, counts, assignment, loader, cycle, group_count):
@@ -118,15 +139,17 @@
     return pl.pallas_call(
         functools.partial(pack_kernel, group_count, cycle),
         in_specs=[pl.BlockSpec(memory_space=pl.ANY)] * 9,
-        out_specs=[pl.BlockSpec(memory_space=pl.ANY), pl.BlockSpec(memory_space=pltpu.VMEM)],
+        out_specs=[pl.BlockSpec(memory_space=pl.ANY)] * 2,
         out_shape=[packed, jax.ShapeDtypeStruct((8, 128), jnp.int32)],
         scratch_shapes=[pltpu.VMEM(x.shape, x.dtype) for x in small]
         + [
             pltpu.VMEM((KINDS, rows, width), jnp.bfloat16),
             pltpu.VMEM(packed.shape, packed.dtype),
+            pltpu.VMEM((8, 128), jnp.int32),
             pltpu.SemaphoreType.DMA((5,)),
-            pltpu.SemaphoreType.DMA((KINDS, rows // ROW_STEP)),
-            pltpu.SemaphoreType.DMA((cycle, rows // ROW_STEP)),
+            pltpu.SemaphoreType.DMA((KINDS, rows // PACK_STEP)),
+            pltpu.SemaphoreType.DMA((cycle, KINDS + packed.shape[1])),
+            pltpu.SemaphoreType.DMA(()),
         ],
         compiler_params=pltpu.CompilerParams(vmem_limit_bytes=60 * MIB),
         cost_estimate=pl.CostEstimate(flops=12 * rows * width, bytes_accessed=16 * rows * width, transcendentals=rows),
@@ -145,7 +168,8 @@
 def attention_kernel(cycle, boundary_ref, x_ref, *rest):
     o_refs, part_ref = rest[:cycle], rest[cycle]
     side_ref, score_ref, grad_ref, softmax_ref, weighted_ref, score_grad_ref, held_ref = rest[cycle + 1 :]
-    _, heads, kinds, rows, width = x_ref.shape
+    _, _, kinds, rows, width = x_ref.shape
+    heads = HEAD_STEP
     slots = cycle * rows
     scale = HEAD_DIM ** (-0.5)
     boundary = boundary_ref[0:1, 0:1]
@@ -157,9 +181,10 @@
     @pl.when(step == 0)
     def _():
         side_ref[...] = (lax.broadcasted_iota(jnp.int32, side_ref.shape, 0) < boundary).astype(jnp.int32)
+        part_ref[...] = jnp.zeros_like(part_ref)
 
     def operands(h):
-        return [x_ref[:, h, a].reshape(slots, width) for a in range(kinds)]
+        return [x_ref[:, step * heads + h, a].reshape(slots, width) for a in range(kinds)]
 
     def products(h):
         q, k, v, g = operands(h)
@@ -205,7 +230,7 @@
         held_ref[h, 3] = dot(softmax_ref[h], g, 1, 0).astype(jnp.bfloat16)
         for s in range(cycle):
             first = pl.multiple_of(lax.rem(place + cycle - s, cycle) * rows, rows)
-            o_refs[s][h] = held_ref[h, :, pl.ds(first, rows), :]
+            o_refs[s][step * heads + h] = held_ref[h, :, pl.ds(first, rows), :]
         query_part = jnp.sum(query_grad * q.astype(jnp.float32), axis=0, keepdims=True)
         key_part = jnp.sum(key_grad * k.astype(jnp.float32), axis=0, keepdims=True)
         parts = jnp.concatenate([query_part, key_part], axis=0)
@@ -229,10 +254,10 @@
         functools.partial(attention_kernel, cycle),
         grid=(heads // HEAD_STEP,),
         in_specs=[
-            pl.BlockSpec(boundary.shape, lambda h: (0, 0)),
-            pl.BlockSpec((cycle, HEAD_STEP, kinds, rows, width), lambda h: (0, h, 0, 0, 0)),
+            pl.BlockSpec(memory_space=pltpu.VMEM),
+            pl.BlockSpec(memory_space=pltpu.VMEM),
         ],
-        out_specs=[pl.BlockSpec((HEAD_STEP, kinds, rows, width), lambda h: (h, 0, 0, 0))] * cycle
+        out_specs=[pl.BlockSpec(memory_space=pltpu.VMEM)] * cycle
         + [pl.BlockSpec(parts, lambda h: (0, 0, 0))],
         out_shape=[jax.ShapeDtypeStruct((heads, kinds, rows, width), jnp.bfloat16)] * cycle
         + [jax.ShapeDtypeStruct(parts, jnp.float32)],
@@ -255,8 +280,14 @@
     return out[:cycle], out[cycle]
 
 
+def slot_order(cycle):
+    return sorted(range(cycle), key=lambda s: -min(s, cycle - s))
+
+
 def finish_kernel(cycle, *refs):
-    back_refs, raws, gains = refs[:cycle], refs[cycle : cycle + 2], refs[cycle + 2 : cycle + 4]
+    back_refs, raws, gains = [None] * cycle, refs[cycle : cycle + 2], refs[cycle + 2 : cycle + 4]
+    for s, ref in zip(slot_order(cycle), refs):
+        back_refs[s] = ref
     att_ref, dq_ref, dk_ref, dv_ref = refs[cycle + 4 : cycle + 8]
     raw_held, grad_held, raw_sems, grad_sems, copy_sems = refs[cycle + 8 :]
     heads, kinds, rows, _ = back_refs[0].shape
@@ -332,7 +363,7 @@
         compiler_params=pltpu.CompilerParams(vmem_limit_bytes=32 * MIB),
         cost_estimate=pl.CostEstimate(flops=20 * rows * width, bytes_accessed=20 * rows * width, transcendentals=rows),
         name="finish",
-    )(*back, q_raw, k_raw, q_gain, k_gain)
+    )(*(back[s] for s in slot_order(cycle)), q_raw, k_raw, q_gain, k_gain)
 
 
 def respread_kernel(part_ref, o_ref):
@@ -352,10 +383,11 @@
 
 
 def gain_grad_kernel(part_ref, q_gain_ref, k_gain_ref, q_ref, k_ref):
-    cycle, count, _ = part_ref.shape
+    total = jnp.sum(part_ref[...], axis=0)
+    cycle, count, _ = total.shape
     for n, (gain_ref, out_ref) in enumerate(((q_gain_ref, q_ref), (k_gain_ref, k_ref))):
         rows = jnp.concatenate(
-            [part_ref[d, 2 * h + n : 2 * h + n + 1] for d in range(cycle) for h in range(count // 2)], axis=0
+            [total[d, 2 * h + n : 2 * h + n + 1] for d in range(cycle) for h in range(count // 2)], axis=0
         )
         out_ref[...] = rows / gain_ref[...]
 
@@ -386,13 +418,13 @@
         q_raw, k_raw, values, grad_out, q_gain_row, k_gain_row, *tables, cycle, outer * inner * cores
     )
     slots, part = attention(boundary, swap(packed, "blk"), inner * cores)
-    back = [slots[0]] + [
-        lax.ppermute(slots[s], "blk", [(i, (i - s) % cycle) for i in range(cycle)]) for s in range(1, cycle)
-    ]
-
-    part = respread(swap(part, ("y", "c"))[:, : 2 * slots[0].shape[0]], outer)
-    part = respread(swap(part, "z"), cycle)
-    part = swap(part, "blk")
+    back = list(slots)
+    for s in slot_order(cycle)[:-1]:
+        back[s] = lax.ppermute(slots[s], "blk", [(i, (i - s) % cycle) for i in range(cycle)])
+
+    part = respread(swap(part, ("y", "c"))[:, : 2 * slots[0].shape[0]], outer * cycle)
+    part = swap(part, ("z", "blk"))
+    part = part.reshape(outer, cycle, *part.shape[1:])
     return (*finish(back, q_raw, k_raw, q_gain_row, k_gain_row), *gain_grad(part, q_gain, k_gain))
 
 

time: 89.5 us -> 85 us (0.950)
  blocking collectives: 42 us -> 25.3 us
  starting transfers between devices: 25 us -> 33.4 us
  waiting for transfers between devices: 5.83 us -> 11.2 us
    all_to_all x2 -> x1, blocking collectives: 42 us -> 25.3 us  [swap(): return lax.all_to_all(array, axes, 0, 0, tiled=True)]
    all_to_all x2, starting transfers between devices: 17.2 us -> 25 us  [swap(): return lax.all_to_all(array, axes, 0, 0, tiled=True)]
    ppermute x3, waiting for transfers between devices: 0.01 us -> 5.34 us  [body(): lax.ppermute(slots[s], 'blk', [(i, (i - s) % cycle) for i in range(cycle)])]
    pallas_call x1, Pallas kernels: 4.27 us -> 3.35 us  [pack(): pl.pallas_call(functools.partial(pack_kernel, group_count, cycle), in_spe...]
  transfers between devices with their start and end apart: 5 -> 5, of which waited for: 2 -> 4; matrix products, arithmetic and copies ran while one was open for 0% -> 0% of each run, Pallas kernels for 3% -> 3%
where the time goes in v3:
time: 85 us; the launch traced here: 84.5 us
  starting transfers between devices  33.4 us (39%)
  blocking collectives  25.3 us (30%)
  Pallas kernels  13.1 us (15%)
  waiting for transfers between devices  11.2 us (13%)
    all_to_all x1, blocking collectives, swap(): return lax.all_to_all(array, axes, 0, 0, tiled=True)  25.3 us
    all_to_all x2, starting transfers between devices, swap(): return lax.all_to_all(array, axes, 0, 0, tiled=True)  25 us
    ppermute x3, starting transfers between devices, body(): lax.ppermute(slots[s], 'blk', [(i, (i - s) % cycle) for i in range(cycle)])  8.42 us
    pallas_call x1, Pallas kernels, attention(): pl.pallas_call(functools.partial(attention_kernel, cycle), grid=(heads //...  6.28 us
    all_to_all x2, waiting for transfers between devices, swap(): return lax.all_to_all(array, axes, 0, 0, tiled=True)  5.83 us
    ppermute x3, waiting for transfers between devices, body(): lax.ppermute(slots[s], 'blk', [(i, (i - s) % cycle) for i in range(cycle)])  5.34 us
    pallas_call x1, Pallas kernels, pack(): pl.pallas_call(functools.partial(pack_kernel, group_count, cycle), in_spe...  3.35 us
    pallas_call x1, Pallas kernels, finish(): pl.pallas_call(functools.partial(finish_kernel, cycle), in_specs=[whole_b...  2.15 us
  transfers between devices with their start and end apart: 5, of which 4 were waited for; matrix products, arithmetic and copies ran while one was open for 0% of the time, Pallas kernels for 3%

profile of v3, /device:TPU:1, one launch (start us, length us, event | category | flops | bytes accessed | tf_op | source)
XLA Modules:
  0.0 84.5 jit_solution(16852469587421075189)
XLA Ops:
  0.6 3.3 %pack.1 = (bf16[4,4,4,128,128]{4,3,2,1,0:T(8,128)(2,1)}, s32[8,128]{1,0:T(8,128)}) custom-call(s32[4,128]{1,0:T(4,128)} %bitcast.17, s32[4,128]{1,0:T(4,128)} %bitcast.18, s32[4,128]{1,0:T(4,128)} %bitcast.19, f32[1,2048]{1,0:T(1,128)} %bitcast.11, f32[1,2048]{1,0:T(1,128)} %bitcast.14, bf16[128,2048]{1,0:T(8,128)(2,1)} %refs_4_.1, ...), custom_call_target="tpu_custom_call" | custom-call | flops 3145728 | bytes 4194304 | tf_op jit(solution)/shard_map/pack/pallas_call | solution.py:139
  4.0 0.0 copy-start.5
  4.0 25.3 %all_to_all.15.x_ref = bf16[4,4,4,128,128]{4,3,2,1,0:T(8,128)(2,1)S(1)} all-to-all(bf16[4,4,4,128,128]{4,3,2,1,0:T(8,128)(2,1)} %get-tuple-element.20), channel_id=1, replica_groups=mesh['blk'=4,'z'=8,'y'=8,'c'=2] {'blk'}, dimensions={0} | all-to-all | bytes 4194304 | tf_op jit(solution)/shard_map/all_to_all | solution.py:409
  29.3 0.0 copy-done.5
  29.3 0.0 copy-start.3
  29.3 6.3 %attention.1 = (bf16[4,4,128,128]{3,2,1,0:T(8,128)(2,1)S(1)}, bf16[4,4,128,128]{3,2,1,0:T(8,128)(2,1)}, bf16[4,4,128,128]{3,2,1,0:T(8,128)(2,1)}, bf16[4,4,128,128]{3,2,1,0:T(8,128)(2,1)S(1)}, f32[16,32,128]{2,1,0:T(8,128)}) custom-call(s32[8,128]{1,0:T(8,128)S(1)} %copy-done.5, bf16[4,4,4,128,128]{4,3,2,1,0:T(8,128)(2,1)S(1)} %all_to_all.15.x_ref), custom_call_target="tpu_custom_call" | custom-call | flops 1879048192 | bytes 4194304 | tf_op jit(solution)/shard_map/attention/pallas_call | solution.py:253
  35.6 0.8 copy-done.4
  36.4 13.9 %all-to-all-start.1 = ((f32[16,32,128]{2,1,0:T(8,128)}), f32[16,32,128]{2,1,0:T(8,128)S(1)}, u32[]{:S(2)}, u32[]{:S(2)}) async-start(f32[16,32,128]{2,1,0:T(8,128)} %get-tuple-element.29), calls=%async_computation.1 | async-start | bytes 524288 | tf_op jit(solution)/shard_map/all_to_all | solution.py:409
  50.4 2.4 %collective-permute-start = (bf16[4,4,128,128]{3,2,1,0:T(8,128)(2,1)}, bf16[4,4,128,128]{3,2,1,0:T(8,128)(2,1)S(1)}, u32[]{:S(2)}, u32[]{:S(2)}) collective-permute-start(bf16[4,4,128,128]{3,2,1,0:T(8,128)(2,1)} %get-tuple-element.21), channel_id=1, source_target_pairs={{0,256},{128,384},{256,0},{384,128},{1,257},{129,385},{257,1},{385... | collective-permute-start | bytes 1572872 | tf_op jit(solution)/shard_map/ppermute | solution.py:423
  52.8 4.1 %collective-permute-start.1 = (bf16[4,4,128,128]{3,2,1,0:T(8,128)(2,1)}, bf16[4,4,128,128]{3,2,1,0:T(8,128)(2,1)S(1)}, u32[]{:S(2)}, u32[]{:S(2)}) collective-permute-start(bf16[4,4,128,128]{3,2,1,0:T(8,128)(2,1)} %get-tuple-element.22), channel_id=1, source_target_pairs={{0,384},{128,0},{256,128},{384,256},{1,385},{129,1},{257,129},{385... | collective-permute-start | bytes 1572872 | tf_op jit(solution)/shard_map/ppermute | solution.py:423
  56.9 1.9 %collective-permute-start.2 = (bf16[4,4,128,128]{3,2,1,0:T(8,128)(2,1)}, bf16[4,4,128,128]{3,2,1,0:T(8,128)(2,1)S(1)}, u32[]{:S(2)}, u32[]{:S(2)}) collective-permute-start(bf16[4,4,128,128]{3,2,1,0:T(8,128)(2,1)} %copy-done.4), channel_id=1, source_target_pairs={{0,128},{128,256},{256,384},{384,0},{1,129},{129,257},{257,385},{3... | collective-permute-start | bytes 1572872 | tf_op jit(solution)/shard_map/ppermute | solution.py:423
  58.8 3.3 %all-to-all-done.1 = f32[16,32,128]{2,1,0:T(8,128)S(1)} async-done(((f32[16,32,128]{2,1,0:T(8,128)}), f32[16,32,128]{2,1,0:T(8,128)S(1)}, u32[]{:S(2)}, u32[]{:S(2)}) %all-to-all-start.1) | async-done | bytes 262176 | tf_op jit(solution)/shard_map/all_to_all | solution.py:409
  62.1 0.7 respread.1
  62.8 11.0 %all-to-all-start.2 = ((f32[32,8,128]{2,1,0:T(8,128)}), f32[32,8,128]{2,1,0:T(8,128)S(1)}, u32[]{:S(2)}, u32[]{:S(2)}) async-start(f32[32,8,128]{2,1,0:T(8,128)} %respread.1), calls=%async_computation.2 | async-start | bytes 262144 | tf_op jit(solution)/shard_map/all_to_all | solution.py:409
  73.8 0.0 collective-permute-done.refs_0_
  73.8 3.4 %collective-permute-done.1.refs_1_ = bf16[4,4,128,128]{3,2,1,0:T(8,128)(2,1)S(1)} collective-permute-done((bf16[4,4,128,128]{3,2,1,0:T(8,128)(2,1)}, bf16[4,4,128,128]{3,2,1,0:T(8,128)(2,1)S(1)}, u32[]{:S(2)}, u32[]{:S(2)}) %collective-permute-start.1) | collective-permute-done | bytes 524320 | tf_op jit(solution)/shard_map/ppermute | solution.py:423
  77.2 1.9 %collective-permute-done.2.refs_2_ = bf16[4,4,128,128]{3,2,1,0:T(8,128)(2,1)S(1)} collective-permute-done((bf16[4,4,128,128]{3,2,1,0:T(8,128)(2,1)}, bf16[4,4,128,128]{3,2,1,0:T(8,128)(2,1)S(1)}, u32[]{:S(2)}, u32[]{:S(2)}) %collective-permute-start.2) | collective-permute-done | bytes 524320 | tf_op jit(solution)/shard_map/ppermute | solution.py:423
  79.1 0.0 copy-done
  79.2 0.0 copy-done.1
  79.2 0.0 copy-done.2
  79.2 0.0 copy-done.3
  79.2 2.1 %finish.1 = (bf16[128,2048]{1,0:T(8,128)(2,1)}, bf16[128,2048]{1,0:T(8,128)(2,1)}, bf16[128,2048]{1,0:T(8,128)(2,1)}, bf16[128,2048]{1,0:T(8,128)(2,1)}) custom-call(bf16[4,4,128,128]{3,2,1,0:T(8,128)(2,1)S(1)} %collective-permute-done.refs_0_, bf16[4,4,128,128]{3,2,1,0:T(8,128)(2,1)S(1)} %collective-permute-done.1.refs_1_, ...), custom_call_target="tpu_custom_call" | custom-call | flops 5242880 | bytes 5242880 | tf_op jit(solution)/shard_map/finish/pallas_call | solution.py:349
  81.3 2.6 %all-to-all-done.2 = f32[32,8,128]{2,1,0:T(8,128)S(1)} async-done(((f32[32,8,128]{2,1,0:T(8,128)}), f32[32,8,128]{2,1,0:T(8,128)S(1)}, u32[]{:S(2)}, u32[]{:S(2)}) %all-to-all-start.2) | async-done | bytes 131104 | tf_op jit(solution)/shard_map/all_to_all | solution.py:409
  83.9 0.6 gain_grad.1
  (5 shorter events, 0.0 us)
Async XLA Ops:
  4.0 25.3 %copy-start.5 = (s32[8,128]{1,0:T(8,128)S(1)}, s32[8,128]{1,0:T(8,128)}, u32[]{:S(2)}) copy-start(s32[8,128]{1,0:T(8,128)} %get-tuple-element.19.boundary_ref) | copy-start | bytes 12292
  29.3 49.8 %copy-start = (bf16[128,2048]{1,0:T(8,128)(2,1)S(1)}, bf16[128,2048]{1,0:T(8,128)(2,1)}, u32[]{:S(2)}) copy-start(bf16[128,2048]{1,0:T(8,128)(2,1)} %refs_4_.1) | copy-start | bytes 1572868
  29.3 49.8 %copy-start.1 = (bf16[128,2048]{1,0:T(8,128)(2,1)S(1)}, bf16[128,2048]{1,0:T(8,128)(2,1)}, u32[]{:S(2)}) copy-start(bf16[128,2048]{1,0:T(8,128)(2,1)} %refs_5_.3) | copy-start | bytes 1572868
  29.3 49.8 %copy-start.2 = (f32[2048]{0:T(1024)S(1)}, f32[2048]{0:T(1024)}, u32[]{:S(2)}) copy-start(f32[2048]{0:T(1024)} %param.13) | copy-start | bytes 24580
  29.3 49.8 %copy-start.3 = (f32[2048]{0:T(1024)S(1)}, f32[2048]{0:T(1024)}, u32[]{:S(2)}) copy-start(f32[2048]{0:T(1024)} %param.14) | copy-start | bytes 24580
  35.6 0.8 copy-start.4
  36.4 25.6 %all-to-all-start.1 = ((f32[16,32,128]{2,1,0:T(8,128)}), f32[16,32,128]{2,1,0:T(8,128)S(1)}, u32[]{:S(2)}, u32[]{:S(2)}) async-start(f32[16,32,128]{2,1,0:T(8,128)} %get-tuple-element.29), calls=%async_computation.1 | async-start | bytes 524288 | tf_op jit(solution)/shard_map/all_to_all | solution.py:409
  50.4 23.5 %collective-permute-start = (bf16[4,4,128,128]{3,2,1,0:T(8,128)(2,1)}, bf16[4,4,128,128]{3,2,1,0:T(8,128)(2,1)S(1)}, u32[]{:S(2)}, u32[]{:S(2)}) collective-permute-start(bf16[4,4,128,128]{3,2,1,0:T(8,128)(2,1)} %get-tuple-element.21), channel_id=1, source_target_pairs={{0,256},{128,384},{256,0},{384,128},{1,257},{129,385},{257,1},{385... | collective-permute-start | bytes 1572872 | tf_op jit(solution)/shard_map/ppermute | solution.py:423
  52.8 24.4 %collective-permute-start.1 = (bf16[4,4,128,128]{3,2,1,0:T(8,128)(2,1)}, bf16[4,4,128,128]{3,2,1,0:T(8,128)(2,1)S(1)}, u32[]{:S(2)}, u32[]{:S(2)}) collective-permute-start(bf16[4,4,128,128]{3,2,1,0:T(8,128)(2,1)} %get-tuple-element.22), channel_id=1, source_target_pairs={{0,384},{128,0},{256,128},{384,256},{1,385},{129,1},{257,129},{385... | collective-permute-start | bytes 1572872 | tf_op jit(solution)/shard_map/ppermute | solution.py:423
  56.9 22.3 %collective-permute-start.2 = (bf16[4,4,128,128]{3,2,1,0:T(8,128)(2,1)}, bf16[4,4,128,128]{3,2,1,0:T(8,128)(2,1)S(1)}, u32[]{:S(2)}, u32[]{:S(2)}) collective-permute-start(bf16[4,4,128,128]{3,2,1,0:T(8,128)(2,1)} %copy-done.4), channel_id=1, source_target_pairs={{0,128},{128,256},{256,384},{384,0},{1,129},{129,257},{257,385},{3... | collective-permute-start | bytes 1572872 | tf_op jit(solution)/shard_map/ppermute | solution.py:423
  62.8 21.1 %all-to-all-start.2 = ((f32[32,8,128]{2,1,0:T(8,128)}), f32[32,8,128]{2,1,0:T(8,128)S(1)}, u32[]{:S(2)}, u32[]{:S(2)}) async-start(f32[32,8,128]{2,1,0:T(8,128)} %respread.1), calls=%async_computation.2 | async-start | bytes 262144 | tf_op jit(solution)/shard_map/all_to_all | solution.py:409

commit v4 on v3

--- a/solution.py
+++ b/solution.py
@@ -11,10 +11,10 @@
 HEAD_DIM = 128
 KINDS = 4
 PACK_STEP = 128
-ROW_STEP = 64
-HEAD_STEP = 2
+ROW_STEP = 128
+HEAD_STEP = 4
 KEY_STEP = 64
-PART_ROWS = 32
+PART_ROWS = 24
 GROUP_AXES = ("z", "y", "c")
 MIB = 1024 * 1024
 
@@ -289,7 +289,7 @@
     for s, ref in zip(slot_order(cycle), refs):
         back_refs[s] = ref
     att_ref, dq_ref, dk_ref, dv_ref = refs[cycle + 4 : cycle + 8]
-    raw_held, grad_held, raw_sems, grad_sems, copy_sems = refs[cycle + 8 :]
+    grad_held, grad_sems, copy_sems = refs[cycle + 8 :]
     heads, kinds, rows, _ = back_refs[0].shape
     share = heads * HEAD_DIM
     width = share * cycle
@@ -297,10 +297,6 @@
     place = lax.axis_index("blk")
     starts = [pl.multiple_of(lax.rem(place + s, cycle) * share, share) for s in range(cycle)]
 
-    def raw_copy(n, step):
-        block = pl.ds(step * ROW_STEP, ROW_STEP)
-        return pltpu.make_async_copy(raws[n].at[block], raw_held.at[n, block], raw_sems.at[n, step])
-
     def grad_copy(n, step):
         block = pl.ds(step * ROW_STEP, ROW_STEP)
         return pltpu.make_async_copy(
@@ -312,16 +308,12 @@
         return pltpu.make_async_copy(back_refs[s].at[h, 3 * n], target, copy_sems.at[n, s, h])
 
     plain = [plain_copy(n, s, h) for n in range(2) for s in range(cycle) for h in range(heads)]
-    for step in range(steps):
-        for n in range(2):
-            raw_copy(n, step).start()
     for copy in plain:
         copy.start()
     for step in range(steps):
         block = slice(step * ROW_STEP, (step + 1) * ROW_STEP)
         for n in range(2):
-            raw_copy(n, step).wait()
-            raw = [raw_held[n, block, pl.ds(start, share)].astype(jnp.float32) for start in starts]
+            raw = [raws[n][block, pl.ds(start, share)].astype(jnp.float32) for start in starts]
             grad = [
                 jnp.concatenate([back[h, 1 + n, block] for h in range(heads)], axis=1).astype(jnp.float32)
                 * gains[n][:, pl.ds(start, share)]
@@ -348,15 +340,11 @@
     steps = rows // ROW_STEP
     return pl.pallas_call(
         functools.partial(finish_kernel, cycle),
-        in_specs=[whole_block(back[0].shape)] * cycle
-        + [pl.BlockSpec(memory_space=pl.ANY)] * 2
-        + [whole_block((1, width))] * 2,
+        in_specs=[whole_block(back[0].shape)] * cycle + [whole_block((rows, width))] * 2 + [whole_block((1, width))] * 2,
         out_specs=[pl.BlockSpec(memory_space=pl.ANY)] * 4,
         out_shape=[jax.ShapeDtypeStruct((rows, width), jnp.bfloat16)] * 4,
         scratch_shapes=[
             pltpu.VMEM((2, rows, width), jnp.bfloat16),
-            pltpu.VMEM((2, rows, width), jnp.bfloat16),
-            pltpu.SemaphoreType.DMA((2, steps)),
             pltpu.SemaphoreType.DMA((2, steps)),
             pltpu.SemaphoreType.DMA((2, cycle, heads)),
         ],

time: 85 us -> 83.5 us (0.982); the launches traced: 84.5 us -> 82 us
  waiting for transfers between devices: 11.2 us -> 9.09 us
    all_to_all x2, waiting for transfers between devices: 5.83 us -> 2.04 us  [swap(): return lax.all_to_all(array, axes, 0, 0, tiled=True)]
    ppermute x3, waiting for transfers between devices: 5.34 us -> 7.05 us  [body(): lax.ppermute(slots[s], 'blk', [(i, (i - s) % cycle) for i in range(cycle)])]
where the time goes in v4:
time: 83.5 us; the launch traced here: 82 us
  starting transfers between devices  33.4 us (40%)
  blocking collectives  25.3 us (30%)
  Pallas kernels  12.6 us (15%)
  waiting for transfers between devices  9.09 us (11%)
    all_to_all x1, blocking collectives, swap(): return lax.all_to_all(array, axes, 0, 0, tiled=True)  25.3 us
    all_to_all x2, starting transfers between devices, swap(): return lax.all_to_all(array, axes, 0, 0, tiled=True)  25 us
    ppermute x3, starting transfers between devices, body(): lax.ppermute(slots[s], 'blk', [(i, (i - s) % cycle) for i in range(cycle)])  8.41 us
    ppermute x3, waiting for transfers between devices, body(): lax.ppermute(slots[s], 'blk', [(i, (i - s) % cycle) for i in range(cycle)])  7.05 us
    pallas_call x1, Pallas kernels, attention(): pl.pallas_call(functools.partial(attention_kernel, cycle), grid=(heads //...  5.84 us
    pallas_call x1, Pallas kernels, pack(): pl.pallas_call(functools.partial(pack_kernel, group_count, cycle), in_spe...  3.35 us
    pallas_call x1, Pallas kernels, finish(): pl.pallas_call(functools.partial(finish_kernel, cycle), in_specs=[whole_b...  2.12 us
    all_to_all x2, waiting for transfers between devices, swap(): return lax.all_to_all(array, axes, 0, 0, tiled=True)  2.04 us
  transfers between devices with their start and end apart: 5, of which 4 were waited for; matrix products, arithmetic and copies ran while one was open for 0% of the time, Pallas kernels for 3%

profile of v4, /device:TPU:1, one launch (start us, length us, event | category | flops | bytes accessed | tf_op | source)
XLA Modules:
  0.0 82.0 jit_solution(7574425144495044977)
XLA Ops:
  0.6 3.3 %pack.1 = (bf16[4,4,4,128,128]{4,3,2,1,0:T(8,128)(2,1)}, s32[8,128]{1,0:T(8,128)}) custom-call(s32[4,128]{1,0:T(4,128)} %bitcast.17, s32[4,128]{1,0:T(4,128)} %bitcast.18, s32[4,128]{1,0:T(4,128)} %bitcast.19, f32[1,2048]{1,0:T(1,128)} %bitcast.11, f32[1,2048]{1,0:T(1,128)} %bitcast.14, bf16[128,2048]{1,0:T(8,128)(2,1)} %refs_4_.1, ...), custom_call_target="tpu_custom_call" | custom-call | flops 3145728 | bytes 4194304 | tf_op jit(solution)/shard_map/pack/pallas_call | solution.py:139
  4.0 0.0 copy-start.5
  4.0 25.3 %all_to_all.15.x_ref = bf16[4,4,4,128,128]{4,3,2,1,0:T(8,128)(2,1)S(1)} all-to-all(bf16[4,4,4,128,128]{4,3,2,1,0:T(8,128)(2,1)} %get-tuple-element.20), channel_id=1, replica_groups=mesh['blk'=4,'z'=8,'y'=8,'c'=2] {'blk'}, dimensions={0} | all-to-all | bytes 4194304 | tf_op jit(solution)/shard_map/all_to_all | solution.py:397
  29.3 0.0 copy-done.5
  29.3 0.0 copy-start.3
  29.3 5.8 %attention.1 = (bf16[4,4,128,128]{3,2,1,0:T(8,128)(2,1)S(1)}, bf16[4,4,128,128]{3,2,1,0:T(8,128)(2,1)}, bf16[4,4,128,128]{3,2,1,0:T(8,128)(2,1)}, bf16[4,4,128,128]{3,2,1,0:T(8,128)(2,1)S(1)}, f32[16,24,128]{2,1,0:T(8,128)}) custom-call(s32[8,128]{1,0:T(8,128)S(1)} %copy-done.5, bf16[4,4,4,128,128]{4,3,2,1,0:T(8,128)(2,1)S(1)} %all_to_all.15.x_ref), custom_call_target="tpu_custom_call" | custom-call | flops 1879048192 | bytes 4194304 | tf_op jit(solution)/shard_map/attention/pallas_call | solution.py:253
  35.2 0.8 copy-done.4
  36.0 14.0 %all-to-all-start.1 = ((f32[16,24,128]{2,1,0:T(8,128)}), f32[16,24,128]{2,1,0:T(8,128)S(1)}, u32[]{:S(2)}, u32[]{:S(2)}) async-start(f32[16,24,128]{2,1,0:T(8,128)} %get-tuple-element.29), calls=%async_computation.1 | async-start | bytes 393216 | tf_op jit(solution)/shard_map/all_to_all | solution.py:397
  49.9 2.5 %collective-permute-start = (bf16[4,4,128,128]{3,2,1,0:T(8,128)(2,1)}, bf16[4,4,128,128]{3,2,1,0:T(8,128)(2,1)S(1)}, u32[]{:S(2)}, u32[]{:S(2)}) collective-permute-start(bf16[4,4,128,128]{3,2,1,0:T(8,128)(2,1)} %get-tuple-element.21), channel_id=1, source_target_pairs={{0,256},{128,384},{256,0},{384,128},{1,257},{129,385},{257,1},{385... | collective-permute-start | bytes 1572872 | tf_op jit(solution)/shard_map/ppermute | solution.py:411
  52.4 4.0 %collective-permute-start.1 = (bf16[4,4,128,128]{3,2,1,0:T(8,128)(2,1)}, bf16[4,4,128,128]{3,2,1,0:T(8,128)(2,1)S(1)}, u32[]{:S(2)}, u32[]{:S(2)}) collective-permute-start(bf16[4,4,128,128]{3,2,1,0:T(8,128)(2,1)} %get-tuple-element.22), channel_id=1, source_target_pairs={{0,384},{128,0},{256,128},{384,256},{1,385},{129,1},{257,129},{385... | collective-permute-start | bytes 1572872 | tf_op jit(solution)/shard_map/ppermute | solution.py:411
  56.4 1.9 %collective-permute-start.2 = (bf16[4,4,128,128]{3,2,1,0:T(8,128)(2,1)}, bf16[4,4,128,128]{3,2,1,0:T(8,128)(2,1)S(1)}, u32[]{:S(2)}, u32[]{:S(2)}) collective-permute-start(bf16[4,4,128,128]{3,2,1,0:T(8,128)(2,1)} %copy-done.4), channel_id=1, source_target_pairs={{0,128},{128,256},{256,384},{384,0},{1,129},{129,257},{257,385},{3... | collective-permute-start | bytes 1572872 | tf_op jit(solution)/shard_map/ppermute | solution.py:411
  58.4 1.9 %all-to-all-done.1 = f32[16,24,128]{2,1,0:T(8,128)S(1)} async-done(((f32[16,24,128]{2,1,0:T(8,128)}), f32[16,24,128]{2,1,0:T(8,128)S(1)}, u32[]{:S(2)}, u32[]{:S(2)}) %all-to-all-start.1) | async-done | bytes 196640 | tf_op jit(solution)/shard_map/all_to_all | solution.py:397
  60.3 0.7 respread.1
  60.9 11.0 %all-to-all-start.2 = ((f32[32,8,128]{2,1,0:T(8,128)}), f32[32,8,128]{2,1,0:T(8,128)S(1)}, u32[]{:S(2)}, u32[]{:S(2)}) async-start(f32[32,8,128]{2,1,0:T(8,128)} %respread.1), calls=%async_computation.2 | async-start | bytes 262144 | tf_op jit(solution)/shard_map/all_to_all | solution.py:397
  72.0 0.0 collective-permute-done.refs_0_
  72.0 5.0 %collective-permute-done.1.refs_1_ = bf16[4,4,128,128]{3,2,1,0:T(8,128)(2,1)S(1)} collective-permute-done((bf16[4,4,128,128]{3,2,1,0:T(8,128)(2,1)}, bf16[4,4,128,128]{3,2,1,0:T(8,128)(2,1)S(1)}, u32[]{:S(2)}, u32[]{:S(2)}) %collective-permute-start.1) | collective-permute-done | bytes 524320 | tf_op jit(solution)/shard_map/ppermute | solution.py:411
  77.0 2.0 %collective-permute-done.2.refs_2_ = bf16[4,4,128,128]{3,2,1,0:T(8,128)(2,1)S(1)} collective-permute-done((bf16[4,4,128,128]{3,2,1,0:T(8,128)(2,1)}, bf16[4,4,128,128]{3,2,1,0:T(8,128)(2,1)S(1)}, u32[]{:S(2)}, u32[]{:S(2)}) %collective-permute-start.2) | collective-permute-done | bytes 524320 | tf_op jit(solution)/shard_map/ppermute | solution.py:411
  79.0 0.0 copy-done
  79.0 0.0 copy-done.1
  79.0 0.0 copy-done.2
  79.0 0.0 copy-done.3
  79.1 2.1 %finish.1 = (bf16[128,2048]{1,0:T(8,128)(2,1)}, bf16[128,2048]{1,0:T(8,128)(2,1)}, bf16[128,2048]{1,0:T(8,128)(2,1)}, bf16[128,2048]{1,0:T(8,128)(2,1)}) custom-call(bf16[4,4,128,128]{3,2,1,0:T(8,128)(2,1)S(1)} %collective-permute-done.refs_0_, bf16[4,4,128,128]{3,2,1,0:T(8,128)(2,1)S(1)} %collective-permute-done.1.refs_1_, ...), custom_call_target="tpu_custom_call" | custom-call | flops 5242880 | bytes 5242880 | tf_op jit(solution)/shard_map/finish/pallas_call | solution.py:341
  81.2 0.2 all-to-all-done.2
  81.3 0.6 gain_grad.1
  (5 shorter events, 0.0 us)
Async XLA Ops:
  4.0 25.3 %copy-start.5 = (s32[8,128]{1,0:T(8,128)S(1)}, s32[8,128]{1,0:T(8,128)}, u32[]{:S(2)}) copy-start(s32[8,128]{1,0:T(8,128)} %get-tuple-element.19.boundary_ref) | copy-start | bytes 12292
  29.3 49.7 %copy-start = (bf16[128,2048]{1,0:T(8,128)(2,1)S(1)}, bf16[128,2048]{1,0:T(8,128)(2,1)}, u32[]{:S(2)}) copy-start(bf16[128,2048]{1,0:T(8,128)(2,1)} %refs_4_.1) | copy-start | bytes 1572868
  29.3 49.7 %copy-start.1 = (bf16[128,2048]{1,0:T(8,128)(2,1)S(1)}, bf16[128,2048]{1,0:T(8,128)(2,1)}, u32[]{:S(2)}) copy-start(bf16[128,2048]{1,0:T(8,128)(2,1)} %refs_5_.3) | copy-start | bytes 1572868
  29.3 49.7 %copy-start.2 = (f32[2048]{0:T(1024)S(1)}, f32[2048]{0:T(1024)}, u32[]{:S(2)}) copy-start(f32[2048]{0:T(1024)} %param.13) | copy-start | bytes 24580
  29.3 49.7 %copy-start.3 = (f32[2048]{0:T(1024)S(1)}, f32[2048]{0:T(1024)}, u32[]{:S(2)}) copy-start(f32[2048]{0:T(1024)} %param.14) | copy-start | bytes 24580
  35.2 0.8 copy-start.4
  36.0 24.3 %all-to-all-start.1 = ((f32[16,24,128]{2,1,0:T(8,128)}), f32[16,24,128]{2,1,0:T(8,128)S(1)}, u32[]{:S(2)}, u32[]{:S(2)}) async-start(f32[16,24,128]{2,1,0:T(8,128)} %get-tuple-element.29), calls=%async_computation.1 | async-start | bytes 393216 | tf_op jit(solution)/shard_map/all_to_all | solution.py:397
  49.9 22.0 %collective-permute-start = (bf16[4,4,128,128]{3,2,1,0:T(8,128)(2,1)}, bf16[4,4,128,128]{3,2,1,0:T(8,128)(2,1)S(1)}, u32[]{:S(2)}, u32[]{:S(2)}) collective-permute-start(bf16[4,4,128,128]{3,2,1,0:T(8,128)(2,1)} %get-tuple-element.21), channel_id=1, source_target_pairs={{0,256},{128,384},{256,0},{384,128},{1,257},{129,385},{257,1},{385... | collective-permute-start | bytes 1572872 | tf_op jit(solution)/shard_map/ppermute | solution.py:411
  52.4 24.6 %collective-permute-start.1 = (bf16[4,4,128,128]{3,2,1,0:T(8,128)(2,1)}, bf16[4,4,128,128]{3,2,1,0:T(8,128)(2,1)S(1)}, u32[]{:S(2)}, u32[]{:S(2)}) collective-permute-start(bf16[4,4,128,128]{3,2,1,0:T(8,128)(2,1)} %get-tuple-element.22), channel_id=1, source_target_pairs={{0,384},{128,0},{256,128},{384,256},{1,385},{129,1},{257,129},{385... | collective-permute-start | bytes 1572872 | tf_op jit(solution)/shard_map/ppermute | solution.py:411
  56.4 22.6 %collective-permute-start.2 = (bf16[4,4,128,128]{3,2,1,0:T(8,128)(2,1)}, bf16[4,4,128,128]{3,2,1,0:T(8,128)(2,1)S(1)}, u32[]{:S(2)}, u32[]{:S(2)}) collective-permute-start(bf16[4,4,128,128]{3,2,1,0:T(8,128)(2,1)} %copy-done.4), channel_id=1, source_target_pairs={{0,128},{128,256},{256,384},{384,0},{1,129},{129,257},{257,385},{3... | collective-permute-start | bytes 1572872 | tf_op jit(solution)/shard_map/ppermute | solution.py:411
  60.9 20.4 %all-to-all-start.2 = ((f32[32,8,128]{2,1,0:T(8,128)}), f32[32,8,128]{2,1,0:T(8,128)S(1)}, u32[]{:S(2)}, u32[]{:S(2)}) async-start(f32[32,8,128]{2,1,0:T(8,128)} %respread.1), calls=%async_computation.2 | async-start | bytes 262144 | tf_op jit(solution)/shard_map/all_to_all | solution.py:397

commit v5 on v4

--- a/solution.py
+++ b/solution.py
@@ -355,11 +355,12 @@
 
 
 def respread_kernel(part_ref, o_ref):
-    o_ref[...] = jnp.broadcast_to(jnp.sum(part_ref[...], axis=0, keepdims=True), o_ref.shape)
-
-
-def respread(part, copies):
-    out_shape = (copies,) + part.shape[1:]
+    total = jnp.sum(part_ref[:, : o_ref.shape[1]], axis=0, keepdims=True)
+    o_ref[...] = jnp.broadcast_to(total, o_ref.shape)
+
+
+def respread(part, rows, copies):
+    out_shape = (copies, rows, part.shape[2])
     return pl.pallas_call(
         respread_kernel,
         in_specs=[whole_block(part.shape)],
@@ -410,7 +411,7 @@
     for s in slot_order(cycle)[:-1]:
         back[s] = lax.ppermute(slots[s], "blk", [(i, (i - s) % cycle) for i in range(cycle)])
 
-    part = respread(swap(part, ("y", "c"))[:, : 2 * slots[0].shape[0]], outer * cycle)
+    part = respread(swap(part, ("y", "c")), 2 * slots[0].shape[0], outer * cycle)
     part = swap(part, ("z", "blk"))
     part = part.reshape(outer, cycle, *part.shape[1:])
     return (*finish(back, q_raw, k_raw, q_gain_row, k_gain_row), *gain_grad(part, q_gain, k_gain))

time: 83.5 us -> 83.5 us (level)
  no operation moved by 1% of the time
where the time goes in v5:
time: 83.5 us; the launch traced here: 82 us
  starting transfers between devices  33.4 us (40%)
  blocking collectives  25.3 us (30%)
  Pallas kernels  12.6 us (15%)
  waiting for transfers between devices  9.09 us (11%)
    all_to_all x1, blocking collectives, swap(): return lax.all_to_all(array, axes, 0, 0, tiled=True)  25.3 us
    all_to_all x2, starting transfers between devices, swap(): return lax.all_to_all(array, axes, 0, 0, tiled=True)  25 us
    ppermute x3, starting transfers between devices, body(): lax.ppermute(slots[s], 'blk', [(i, (i - s) % cycle) for i in range(cycle)])  8.41 us
    ppermute x3, waiting for transfers between devices, body(): lax.ppermute(slots[s], 'blk', [(i, (i - s) % cycle) for i in range(cycle)])  7.06 us
    pallas_call x1, Pallas kernels, attention(): pl.pallas_call(functools.partial(attention_kernel, cycle), grid=(heads //...  5.84 us
    pallas_call x1, Pallas kernels, pack(): pl.pallas_call(functools.partial(pack_kernel, group_count, cycle), in_spe...  3.35 us
    pallas_call x1, Pallas kernels, finish(): pl.pallas_call(functools.partial(finish_kernel, cycle), in_specs=[whole_b...  2.12 us
    all_to_all x2, waiting for transfers between devices, swap(): return lax.all_to_all(array, axes, 0, 0, tiled=True)  2.04 us
  transfers between devices with their start and end apart: 5, of which 4 were waited for; matrix products, arithmetic and copies ran while one was open for 0% of the time, Pallas kernels for 3%

profile of v5, /device:TPU:1, one launch (start us, length us, event | category | flops | bytes accessed | tf_op | source)
XLA Modules:
  0.0 82.0 jit_solution(2293310872426633549)
XLA Ops:
  0.6 3.3 %pack.1 = (bf16[4,4,4,128,128]{4,3,2,1,0:T(8,128)(2,1)}, s32[8,128]{1,0:T(8,128)}) custom-call(s32[4,128]{1,0:T(4,128)} %bitcast.17, s32[4,128]{1,0:T(4,128)} %bitcast.18, s32[4,128]{1,0:T(4,128)} %bitcast.19, f32[1,2048]{1,0:T(1,128)} %bitcast.11, f32[1,2048]{1,0:T(1,128)} %bitcast.14, bf16[128,2048]{1,0:T(8,128)(2,1)} %refs_4_.1, ...), custom_call_target="tpu_custom_call" | custom-call | flops 3145728 | bytes 4194304 | tf_op jit(solution)/shard_map/pack/pallas_call | solution.py:139
  4.0 0.0 copy-start.5
  4.0 25.3 %all_to_all.15.x_ref = bf16[4,4,4,128,128]{4,3,2,1,0:T(8,128)(2,1)S(1)} all-to-all(bf16[4,4,4,128,128]{4,3,2,1,0:T(8,128)(2,1)} %get-tuple-element.20), channel_id=1, replica_groups=mesh['blk'=4,'z'=8,'y'=8,'c'=2] {'blk'}, dimensions={0} | all-to-all | bytes 4194304 | tf_op jit(solution)/shard_map/all_to_all | solution.py:398
  29.3 0.0 copy-done.5
  29.3 0.0 copy-start.3
  29.3 5.8 %attention.1 = (bf16[4,4,128,128]{3,2,1,0:T(8,128)(2,1)S(1)}, bf16[4,4,128,128]{3,2,1,0:T(8,128)(2,1)}, bf16[4,4,128,128]{3,2,1,0:T(8,128)(2,1)}, bf16[4,4,128,128]{3,2,1,0:T(8,128)(2,1)S(1)}, f32[16,24,128]{2,1,0:T(8,128)}) custom-call(s32[8,128]{1,0:T(8,128)S(1)} %copy-done.5, bf16[4,4,4,128,128]{4,3,2,1,0:T(8,128)(2,1)S(1)} %all_to_all.15.x_ref), custom_call_target="tpu_custom_call" | custom-call | flops 1879048192 | bytes 4194304 | tf_op jit(solution)/shard_map/attention/pallas_call | solution.py:253
  35.2 0.8 copy-done.4
  36.0 14.0 %all-to-all-start.1 = ((f32[16,24,128]{2,1,0:T(8,128)}), f32[16,24,128]{2,1,0:T(8,128)S(1)}, u32[]{:S(2)}, u32[]{:S(2)}) async-start(f32[16,24,128]{2,1,0:T(8,128)} %get-tuple-element.29), calls=%async_computation.1 | async-start | bytes 393216 | tf_op jit(solution)/shard_map/all_to_all | solution.py:398
  49.9 2.5 %collective-permute-start = (bf16[4,4,128,128]{3,2,1,0:T(8,128)(2,1)}, bf16[4,4,128,128]{3,2,1,0:T(8,128)(2,1)S(1)}, u32[]{:S(2)}, u32[]{:S(2)}) collective-permute-start(bf16[4,4,128,128]{3,2,1,0:T(8,128)(2,1)} %get-tuple-element.21), channel_id=1, source_target_pairs={{0,256},{128,384},{256,0},{384,128},{1,257},{129,385},{257,1},{385... | collective-permute-start | bytes 1572872 | tf_op jit(solution)/shard_map/ppermute | solution.py:412
  52.4 4.0 %collective-permute-start.1 = (bf16[4,4,128,128]{3,2,1,0:T(8,128)(2,1)}, bf16[4,4,128,128]{3,2,1,0:T(8,128)(2,1)S(1)}, u32[]{:S(2)}, u32[]{:S(2)}) collective-permute-start(bf16[4,4,128,128]{3,2,1,0:T(8,128)(2,1)} %get-tuple-element.22), channel_id=1, source_target_pairs={{0,384},{128,0},{256,128},{384,256},{1,385},{129,1},{257,129},{385... | collective-permute-start | bytes 1572872 | tf_op jit(solution)/shard_map/ppermute | solution.py:412
  56.4 1.9 %collective-permute-start.2 = (bf16[4,4,128,128]{3,2,1,0:T(8,128)(2,1)}, bf16[4,4,128,128]{3,2,1,0:T(8,128)(2,1)S(1)}, u32[]{:S(2)}, u32[]{:S(2)}) collective-permute-start(bf16[4,4,128,128]{3,2,1,0:T(8,128)(2,1)} %copy-done.4), channel_id=1, source_target_pairs={{0,128},{128,256},{256,384},{384,0},{1,129},{129,257},{257,385},{3... | collective-permute-start | bytes 1572872 | tf_op jit(solution)/shard_map/ppermute | solution.py:412
  58.4 1.9 %all-to-all-done.1.part_ref = f32[16,24,128]{2,1,0:T(8,128)S(1)} async-done(((f32[16,24,128]{2,1,0:T(8,128)}), f32[16,24,128]{2,1,0:T(8,128)S(1)}, u32[]{:S(2)}, u32[]{:S(2)}) %all-to-all-start.1) | async-done | bytes 196640 | tf_op jit(solution)/shard_map/all_to_all | solution.py:398
  60.3 0.7 respread.1
  60.9 11.0 %all-to-all-start.2 = ((f32[32,8,128]{2,1,0:T(8,128)}), f32[32,8,128]{2,1,0:T(8,128)S(1)}, u32[]{:S(2)}, u32[]{:S(2)}) async-start(f32[32,8,128]{2,1,0:T(8,128)} %respread.1), calls=%async_computation.2 | async-start | bytes 262144 | tf_op jit(solution)/shard_map/all_to_all | solution.py:398
  72.0 0.0 collective-permute-done.refs_0_
  72.0 5.0 %collective-permute-done.1.refs_1_ = bf16[4,4,128,128]{3,2,1,0:T(8,128)(2,1)S(1)} collective-permute-done((bf16[4,4,128,128]{3,2,1,0:T(8,128)(2,1)}, bf16[4,4,128,128]{3,2,1,0:T(8,128)(2,1)S(1)}, u32[]{:S(2)}, u32[]{:S(2)}) %collective-permute-start.1) | collective-permute-done | bytes 524320 | tf_op jit(solution)/shard_map/ppermute | solution.py:412
  77.0 2.0 %collective-permute-done.2.refs_2_ = bf16[4,4,128,128]{3,2,1,0:T(8,128)(2,1)S(1)} collective-permute-done((bf16[4,4,128,128]{3,2,1,0:T(8,128)(2,1)}, bf16[4,4,128,128]{3,2,1,0:T(8,128)(2,1)S(1)}, u32[]{:S(2)}, u32[]{:S(2)}) %collective-permute-start.2) | collective-permute-done | bytes 524320 | tf_op jit(solution)/shard_map/ppermute | solution.py:412
  79.0 0.0 copy-done
  79.0 0.0 copy-done.1
  79.0 0.0 copy-done.2
  79.0 0.0 copy-done.3
  79.1 2.1 %finish.1 = (bf16[128,2048]{1,0:T(8,128)(2,1)}, bf16[128,2048]{1,0:T(8,128)(2,1)}, bf16[128,2048]{1,0:T(8,128)(2,1)}, bf16[128,2048]{1,0:T(8,128)(2,1)}) custom-call(bf16[4,4,128,128]{3,2,1,0:T(8,128)(2,1)S(1)} %collective-permute-done.refs_0_, bf16[4,4,128,128]{3,2,1,0:T(8,128)(2,1)S(1)} %collective-permute-done.1.refs_1_, ...), custom_call_target="tpu_custom_call" | custom-call | flops 5242880 | bytes 5242880 | tf_op jit(solution)/shard_map/finish/pallas_call | solution.py:341
  81.2 0.1 all-to-all-done.2
  81.3 0.6 gain_grad.1
  (4 shorter events, 0.0 us)
Async XLA Ops:
  4.0 25.3 %copy-start.5 = (s32[8,128]{1,0:T(8,128)S(1)}, s32[8,128]{1,0:T(8,128)}, u32[]{:S(2)}) copy-start(s32[8,128]{1,0:T(8,128)} %get-tuple-element.19.boundary_ref) | copy-start | bytes 12292
  29.3 49.7 %copy-start = (bf16[128,2048]{1,0:T(8,128)(2,1)S(1)}, bf16[128,2048]{1,0:T(8,128)(2,1)}, u32[]{:S(2)}) copy-start(bf16[128,2048]{1,0:T(8,128)(2,1)} %refs_4_.1) | copy-start | bytes 1572868
  29.3 49.7 %copy-start.1 = (bf16[128,2048]{1,0:T(8,128)(2,1)S(1)}, bf16[128,2048]{1,0:T(8,128)(2,1)}, u32[]{:S(2)}) copy-start(bf16[128,2048]{1,0:T(8,128)(2,1)} %refs_5_.3) | copy-start | bytes 1572868
  29.3 49.7 %copy-start.2 = (f32[2048]{0:T(1024)S(1)}, f32[2048]{0:T(1024)}, u32[]{:S(2)}) copy-start(f32[2048]{0:T(1024)} %param.13) | copy-start | bytes 24580
  29.3 49.7 %copy-start.3 = (f32[2048]{0:T(1024)S(1)}, f32[2048]{0:T(1024)}, u32[]{:S(2)}) copy-start(f32[2048]{0:T(1024)} %param.14) | copy-start | bytes 24580
  35.2 0.8 copy-start.4
  36.0 24.3 %all-to-all-start.1 = ((f32[16,24,128]{2,1,0:T(8,128)}), f32[16,24,128]{2,1,0:T(8,128)S(1)}, u32[]{:S(2)}, u32[]{:S(2)}) async-start(f32[16,24,128]{2,1,0:T(8,128)} %get-tuple-element.29), calls=%async_computation.1 | async-start | bytes 393216 | tf_op jit(solution)/shard_map/all_to_all | solution.py:398
  49.9 22.0 %collective-permute-start = (bf16[4,4,128,128]{3,2,1,0:T(8,128)(2,1)}, bf16[4,4,128,128]{3,2,1,0:T(8,128)(2,1)S(1)}, u32[]{:S(2)}, u32[]{:S(2)}) collective-permute-start(bf16[4,4,128,128]{3,2,1,0:T(8,128)(2,1)} %get-tuple-element.21), channel_id=1, source_target_pairs={{0,256},{128,384},{256,0},{384,128},{1,257},{129,385},{257,1},{385... | collective-permute-start | bytes 1572872 | tf_op jit(solution)/shard_map/ppermute | solution.py:412
  52.4 24.6 %collective-permute-start.1 = (bf16[4,4,128,128]{3,2,1,0:T(8,128)(2,1)}, bf16[4,4,128,128]{3,2,1,0:T(8,128)(2,1)S(1)}, u32[]{:S(2)}, u32[]{:S(2)}) collective-permute-start(bf16[4,4,128,128]{3,2,1,0:T(8,128)(2,1)} %get-tuple-element.22), channel_id=1, source_target_pairs={{0,384},{128,0},{256,128},{384,256},{1,385},{129,1},{257,129},{385... | collective-permute-start | bytes 1572872 | tf_op jit(solution)/shard_map/ppermute | solution.py:412
  56.4 22.6 %collective-permute-start.2 = (bf16[4,4,128,128]{3,2,1,0:T(8,128)(2,1)}, bf16[4,4,128,128]{3,2,1,0:T(8,128)(2,1)S(1)}, u32[]{:S(2)}, u32[]{:S(2)}) collective-permute-start(bf16[4,4,128,128]{3,2,1,0:T(8,128)(2,1)} %copy-done.4), channel_id=1, source_target_pairs={{0,128},{128,256},{256,384},{384,0},{1,129},{129,257},{257,385},{3... | collective-permute-start | bytes 1572872 | tf_op jit(solution)/shard_map/ppermute | solution.py:412
  60.9 20.4 %all-to-all-start.2 = ((f32[32,8,128]{2,1,0:T(8,128)}), f32[32,8,128]{2,1,0:T(8,128)S(1)}, u32[]{:S(2)}, u32[]{:S(2)}) async-start(f32[32,8,128]{2,1,0:T(8,128)} %respread.1), calls=%async_computation.2 | async-start | bytes 262144 | tf_op jit(solution)/shard_map/all_to_all | solution.py:398

commit v6 on v5

--- a/solution.py
+++ b/solution.py
@@ -12,7 +12,6 @@
 KINDS = 4
 PACK_STEP = 128
 ROW_STEP = 128
-HEAD_STEP = 4
 KEY_STEP = 64
 PART_ROWS = 24
 GROUP_AXES = ("z", "y", "c")
@@ -168,23 +167,19 @@
 def attention_kernel(cycle, boundary_ref, x_ref, *rest):
     o_refs, part_ref = rest[:cycle], rest[cycle]
     side_ref, score_ref, grad_ref, softmax_ref, weighted_ref, score_grad_ref, held_ref = rest[cycle + 1 :]
-    _, _, kinds, rows, width = x_ref.shape
-    heads = HEAD_STEP
+    _, heads, kinds, rows, width = x_ref.shape
     slots = cycle * rows
     scale = HEAD_DIM ** (-0.5)
     boundary = boundary_ref[0:1, 0:1]
-    step = pl.program_id(0)
     place = lax.axis_index("blk")
     key_steps = [slice(j, j + KEY_STEP) for j in range(0, slots, KEY_STEP)]
     query_side = (lax.broadcasted_iota(jnp.int32, (1, slots), 1) < boundary).astype(jnp.int32)
 
-    @pl.when(step == 0)
-    def _():
-        side_ref[...] = (lax.broadcasted_iota(jnp.int32, side_ref.shape, 0) < boundary).astype(jnp.int32)
-        part_ref[...] = jnp.zeros_like(part_ref)
+    side_ref[...] = (lax.broadcasted_iota(jnp.int32, side_ref.shape, 0) < boundary).astype(jnp.int32)
+    part_ref[...] = jnp.zeros_like(part_ref)
 
     def operands(h):
-        return [x_ref[:, step * heads + h, a].reshape(slots, width) for a in range(kinds)]
+        return [x_ref[:, h, a].reshape(slots, width) for a in range(kinds)]
 
     def products(h):
         q, k, v, g = operands(h)
@@ -230,11 +225,11 @@
         held_ref[h, 3] = dot(softmax_ref[h], g, 1, 0).astype(jnp.bfloat16)
         for s in range(cycle):
             first = pl.multiple_of(lax.rem(place + cycle - s, cycle) * rows, rows)
-            o_refs[s][step * heads + h] = held_ref[h, :, pl.ds(first, rows), :]
+            o_refs[s][h] = held_ref[h, :, pl.ds(first, rows), :]
         query_part = jnp.sum(query_grad * q.astype(jnp.float32), axis=0, keepdims=True)
         key_part = jnp.sum(key_grad * k.astype(jnp.float32), axis=0, keepdims=True)
         parts = jnp.concatenate([query_part, key_part], axis=0)
-        at = pl.ds(2 * (step * heads + h), 2)
+        at = slice(2 * h, 2 * h + 2)
         part_ref[:, at, :] = jnp.broadcast_to(parts, (part_ref.shape[0], 2, width))
 
     top = products(0)
@@ -249,16 +244,15 @@
     cycle, heads, kinds, rows, width = arrived.shape
     slots = cycle * rows
     parts = (copies, PART_ROWS, width)
-    square = (HEAD_STEP, slots, slots)
+    square = (heads, slots, slots)
     out = pl.pallas_call(
         functools.partial(attention_kernel, cycle),
-        grid=(heads // HEAD_STEP,),
         in_specs=[
             pl.BlockSpec(memory_space=pltpu.VMEM),
             pl.BlockSpec(memory_space=pltpu.VMEM),
         ],
         out_specs=[pl.BlockSpec(memory_space=pltpu.VMEM)] * cycle
-        + [pl.BlockSpec(parts, lambda h: (0, 0, 0))],
+        + [pl.BlockSpec(memory_space=pltpu.VMEM)],
         out_shape=[jax.ShapeDtypeStruct((heads, kinds, rows, width), jnp.bfloat16)] * cycle
         + [jax.ShapeDtypeStruct(parts, jnp.float32)],
         scratch_shapes=[
@@ -268,7 +262,7 @@
             pltpu.VMEM(square, jnp.bfloat16),
             pltpu.VMEM(square, jnp.bfloat16),
             pltpu.VMEM(square, jnp.bfloat16),
-            pltpu.VMEM((HEAD_STEP, kinds, slots, width), jnp.bfloat16),
+            pltpu.VMEM((heads, kinds, slots, width), jnp.bfloat16),
         ],
         compiler_params=pltpu.CompilerParams(vmem_limit_bytes=32 * MIB),
         cost_estimate=pl.CostEstimate(

time: 83.5 us -> 83.5 us (level)
  no operation moved by 1% of the time
where the time goes in v6:
time: 83.5 us; the launch traced here: 82 us
  starting transfers between devices  33.4 us (40%)
  blocking collectives  25.3 us (30%)
  Pallas kernels  12.6 us (15%)
  waiting for transfers between devices  9.09 us (11%)
    all_to_all x1, blocking collectives, swap(): return lax.all_to_all(array, axes, 0, 0, tiled=True)  25.3 us
    all_to_all x2, starting transfers between devices, swap(): return lax.all_to_all(array, axes, 0, 0, tiled=True)  25 us
    ppermute x3, starting transfers between devices, body(): lax.ppermute(slots[s], 'blk', [(i, (i - s) % cycle) for i in range(cycle)])  8.41 us
    ppermute x3, waiting for transfers between devices, body(): lax.ppermute(slots[s], 'blk', [(i, (i - s) % cycle) for i in range(cycle)])  7.06 us
    pallas_call x1, Pallas kernels, attention(): pl.pallas_call(functools.partial(attention_kernel, cycle), in_specs=[pl.B...  5.84 us
    pallas_call x1, Pallas kernels, pack(): pl.pallas_call(functools.partial(pack_kernel, group_count, cycle), in_spe...  3.35 us
    pallas_call x1, Pallas kernels, finish(): pl.pallas_call(functools.partial(finish_kernel, cycle), in_specs=[whole_b...  2.12 us
    all_to_all x2, waiting for transfers between devices, swap(): return lax.all_to_all(array, axes, 0, 0, tiled=True)  2.04 us
  transfers between devices with their start and end apart: 5, of which 4 were waited for; matrix products, arithmetic and copies ran while one was open for 0% of the time, Pallas kernels for 3%

profile of v6, /device:TPU:1, one launch (start us, length us, event | category | flops | bytes accessed | tf_op | source)
XLA Modules:
  0.0 82.0 jit_solution(2293310872426633549)
XLA Ops:
  0.6 3.3 %pack.1 = (bf16[4,4,4,128,128]{4,3,2,1,0:T(8,128)(2,1)}, s32[8,128]{1,0:T(8,128)}) custom-call(s32[4,128]{1,0:T(4,128)} %bitcast.17, s32[4,128]{1,0:T(4,128)} %bitcast.18, s32[4,128]{1,0:T(4,128)} %bitcast.19, f32[1,2048]{1,0:T(1,128)} %bitcast.11, f32[1,2048]{1,0:T(1,128)} %bitcast.14, bf16[128,2048]{1,0:T(8,128)(2,1)} %refs_4_.1, ...), custom_call_target="tpu_custom_call" | custom-call | flops 3145728 | bytes 4194304 | tf_op jit(solution)/shard_map/pack/pallas_call | solution.py:138
  4.0 0.0 copy-start.5
  4.0 25.3 %all_to_all.15.x_ref = bf16[4,4,4,128,128]{4,3,2,1,0:T(8,128)(2,1)S(1)} all-to-all(bf16[4,4,4,128,128]{4,3,2,1,0:T(8,128)(2,1)} %get-tuple-element.20), channel_id=1, replica_groups=mesh['blk'=4,'z'=8,'y'=8,'c'=2] {'blk'}, dimensions={0} | all-to-all | bytes 4194304 | tf_op jit(solution)/shard_map/all_to_all | solution.py:392
  29.3 0.0 copy-done.5
  29.3 0.0 copy-start.3
  29.3 5.8 %attention.1 = (bf16[4,4,128,128]{3,2,1,0:T(8,128)(2,1)S(1)}, bf16[4,4,128,128]{3,2,1,0:T(8,128)(2,1)}, bf16[4,4,128,128]{3,2,1,0:T(8,128)(2,1)}, bf16[4,4,128,128]{3,2,1,0:T(8,128)(2,1)S(1)}, f32[16,24,128]{2,1,0:T(8,128)}) custom-call(s32[8,128]{1,0:T(8,128)S(1)} %copy-done.5, bf16[4,4,4,128,128]{4,3,2,1,0:T(8,128)(2,1)S(1)} %all_to_all.15.x_ref), custom_call_target="tpu_custom_call" | custom-call | flops 1879048192 | bytes 4194304 | tf_op jit(solution)/shard_map/attention/pallas_call | solution.py:248
  35.2 0.8 copy-done.4
  36.0 14.0 %all-to-all-start.1 = ((f32[16,24,128]{2,1,0:T(8,128)}), f32[16,24,128]{2,1,0:T(8,128)S(1)}, u32[]{:S(2)}, u32[]{:S(2)}) async-start(f32[16,24,128]{2,1,0:T(8,128)} %get-tuple-element.29), calls=%async_computation.1 | async-start | bytes 393216 | tf_op jit(solution)/shard_map/all_to_all | solution.py:392
  49.9 2.5 %collective-permute-start = (bf16[4,4,128,128]{3,2,1,0:T(8,128)(2,1)}, bf16[4,4,128,128]{3,2,1,0:T(8,128)(2,1)S(1)}, u32[]{:S(2)}, u32[]{:S(2)}) collective-permute-start(bf16[4,4,128,128]{3,2,1,0:T(8,128)(2,1)} %get-tuple-element.21), channel_id=1, source_target_pairs={{0,256},{128,384},{256,0},{384,128},{1,257},{129,385},{257,1},{385... | collective-permute-start | bytes 1572872 | tf_op jit(solution)/shard_map/ppermute | solution.py:406
  52.4 4.0 %collective-permute-start.1 = (bf16[4,4,128,128]{3,2,1,0:T(8,128)(2,1)}, bf16[4,4,128,128]{3,2,1,0:T(8,128)(2,1)S(1)}, u32[]{:S(2)}, u32[]{:S(2)}) collective-permute-start(bf16[4,4,128,128]{3,2,1,0:T(8,128)(2,1)} %get-tuple-element.22), channel_id=1, source_target_pairs={{0,384},{128,0},{256,128},{384,256},{1,385},{129,1},{257,129},{385... | collective-permute-start | bytes 1572872 | tf_op jit(solution)/shard_map/ppermute | solution.py:406
  56.4 1.9 %collective-permute-start.2 = (bf16[4,4,128,128]{3,2,1,0:T(8,128)(2,1)}, bf16[4,4,128,128]{3,2,1,0:T(8,128)(2,1)S(1)}, u32[]{:S(2)}, u32[]{:S(2)}) collective-permute-start(bf16[4,4,128,128]{3,2,1,0:T(8,128)(2,1)} %copy-done.4), channel_id=1, source_target_pairs={{0,128},{128,256},{256,384},{384,0},{1,129},{129,257},{257,385},{3... | collective-permute-start | bytes 1572872 | tf_op jit(solution)/shard_map/ppermute | solution.py:406
  58.4 1.9 %all-to-all-done.1.part_ref = f32[16,24,128]{2,1,0:T(8,128)S(1)} async-done(((f32[16,24,128]{2,1,0:T(8,128)}), f32[16,24,128]{2,1,0:T(8,128)S(1)}, u32[]{:S(2)}, u32[]{:S(2)}) %all-to-all-start.1) | async-done | bytes 196640 | tf_op jit(solution)/shard_map/all_to_all | solution.py:392
  60.3 0.7 respread.1
  60.9 11.0 %all-to-all-start.2 = ((f32[32,8,128]{2,1,0:T(8,128)}), f32[32,8,128]{2,1,0:T(8,128)S(1)}, u32[]{:S(2)}, u32[]{:S(2)}) async-start(f32[32,8,128]{2,1,0:T(8,128)} %respread.1), calls=%async_computation.2 | async-start | bytes 262144 | tf_op jit(solution)/shard_map/all_to_all | solution.py:392
  72.0 0.0 collective-permute-done.refs_0_
  72.0 5.0 %collective-permute-done.1.refs_1_ = bf16[4,4,128,128]{3,2,1,0:T(8,128)(2,1)S(1)} collective-permute-done((bf16[4,4,128,128]{3,2,1,0:T(8,128)(2,1)}, bf16[4,4,128,128]{3,2,1,0:T(8,128)(2,1)S(1)}, u32[]{:S(2)}, u32[]{:S(2)}) %collective-permute-start.1) | collective-permute-done | bytes 524320 | tf_op jit(solution)/shard_map/ppermute | solution.py:406
  77.0 2.0 %collective-permute-done.2.refs_2_ = bf16[4,4,128,128]{3,2,1,0:T(8,128)(2,1)S(1)} collective-permute-done((bf16[4,4,128,128]{3,2,1,0:T(8,128)(2,1)}, bf16[4,4,128,128]{3,2,1,0:T(8,128)(2,1)S(1)}, u32[]{:S(2)}, u32[]{:S(2)}) %collective-permute-start.2) | collective-permute-done | bytes 524320 | tf_op jit(solution)/shard_map/ppermute | solution.py:406
  79.0 0.0 copy-done
  79.0 0.0 copy-done.1
  79.0 0.0 copy-done.2
  79.0 0.0 copy-done.3
  79.1 2.1 %finish.1 = (bf16[128,2048]{1,0:T(8,128)(2,1)}, bf16[128,2048]{1,0:T(8,128)(2,1)}, bf16[128,2048]{1,0:T(8,128)(2,1)}, bf16[128,2048]{1,0:T(8,128)(2,1)}) custom-call(bf16[4,4,128,128]{3,2,1,0:T(8,128)(2,1)S(1)} %collective-permute-done.refs_0_, bf16[4,4,128,128]{3,2,1,0:T(8,128)(2,1)S(1)} %collective-permute-done.1.refs_1_, ...), custom_call_target="tpu_custom_call" | custom-call | flops 5242880 | bytes 5242880 | tf_op jit(solution)/shard_map/finish/pallas_call | solution.py:335
  81.2 0.1 all-to-all-done.2
  81.3 0.6 gain_grad.1
  (4 shorter events, 0.0 us)
Async XLA Ops:
  4.0 25.3 %copy-start.5 = (s32[8,128]{1,0:T(8,128)S(1)}, s32[8,128]{1,0:T(8,128)}, u32[]{:S(2)}) copy-start(s32[8,128]{1,0:T(8,128)} %get-tuple-element.19.boundary_ref) | copy-start | bytes 12292
  29.3 49.7 %copy-start = (bf16[128,2048]{1,0:T(8,128)(2,1)S(1)}, bf16[128,2048]{1,0:T(8,128)(2,1)}, u32[]{:S(2)}) copy-start(bf16[128,2048]{1,0:T(8,128)(2,1)} %refs_4_.1) | copy-start | bytes 1572868
  29.3 49.7 %copy-start.1 = (bf16[128,2048]{1,0:T(8,128)(2,1)S(1)}, bf16[128,2048]{1,0:T(8,128)(2,1)}, u32[]{:S(2)}) copy-start(bf16[128,2048]{1,0:T(8,128)(2,1)} %refs_5_.3) | copy-start | bytes 1572868
  29.3 49.7 %copy-start.2 = (f32[2048]{0:T(1024)S(1)}, f32[2048]{0:T(1024)}, u32[]{:S(2)}) copy-start(f32[2048]{0:T(1024)} %param.13) | copy-start | bytes 24580
  29.3 49.7 %copy-start.3 = (f32[2048]{0:T(1024)S(1)}, f32[2048]{0:T(1024)}, u32[]{:S(2)}) copy-start(f32[2048]{0:T(1024)} %param.14) | copy-start | bytes 24580
  35.2 0.8 copy-start.4
  36.0 24.3 %all-to-all-start.1 = ((f32[16,24,128]{2,1,0:T(8,128)}), f32[16,24,128]{2,1,0:T(8,128)S(1)}, u32[]{:S(2)}, u32[]{:S(2)}) async-start(f32[16,24,128]{2,1,0:T(8,128)} %get-tuple-element.29), calls=%async_computation.1 | async-start | bytes 393216 | tf_op jit(solution)/shard_map/all_to_all | solution.py:392
  49.9 22.0 %collective-permute-start = (bf16[4,4,128,128]{3,2,1,0:T(8,128)(2,1)}, bf16[4,4,128,128]{3,2,1,0:T(8,128)(2,1)S(1)}, u32[]{:S(2)}, u32[]{:S(2)}) collective-permute-start(bf16[4,4,128,128]{3,2,1,0:T(8,128)(2,1)} %get-tuple-element.21), channel_id=1, source_target_pairs={{0,256},{128,384},{256,0},{384,128},{1,257},{129,385},{257,1},{385... | collective-permute-start | bytes 1572872 | tf_op jit(solution)/shard_map/ppermute | solution.py:406
  52.4 24.6 %collective-permute-start.1 = (bf16[4,4,128,128]{3,2,1,0:T(8,128)(2,1)}, bf16[4,4,128,128]{3,2,1,0:T(8,128)(2,1)S(1)}, u32[]{:S(2)}, u32[]{:S(2)}) collective-permute-start(bf16[4,4,128,128]{3,2,1,0:T(8,128)(2,1)} %get-tuple-element.22), channel_id=1, source_target_pairs={{0,384},{128,0},{256,128},{384,256},{1,385},{129,1},{257,129},{385... | collective-permute-start | bytes 1572872 | tf_op jit(solution)/shard_map/ppermute | solution.py:406
  56.4 22.6 %collective-permute-start.2 = (bf16[4,4,128,128]{3,2,1,0:T(8,128)(2,1)}, bf16[4,4,128,128]{3,2,1,0:T(8,128)(2,1)S(1)}, u32[]{:S(2)}, u32[]{:S(2)}) collective-permute-start(bf16[4,4,128,128]{3,2,1,0:T(8,128)(2,1)} %copy-done.4), channel_id=1, source_target_pairs={{0,128},{128,256},{256,384},{384,0},{1,129},{129,257},{257,385},{3... | collective-permute-start | bytes 1572872 | tf_op jit(solution)/shard_map/ppermute | solution.py:406
  60.9 20.4 %all-to-all-start.2 = ((f32[32,8,128]{2,1,0:T(8,128)}), f32[32,8,128]{2,1,0:T(8,128)S(1)}, u32[]{:S(2)}, u32[]{:S(2)}) async-start(f32[32,8,128]{2,1,0:T(8,128)} %respread.1), calls=%async_computation.2 | async-start | bytes 262144 | tf_op jit(solution)/shard_map/all_to_all | solution.py:392
